TPU v7x, 256 devices: a whole 4x4x8 slice. The times are simulated.
256 devices in a mesh: ctx: 32 (over x, z), head: 8 (over y, core).
Axes of the slice: x: 4, y: 4, z: 8, core: 2. Of those that a mesh axis runs over, the one named last changes fastest.
Arguments:
- queries: bfloat16 [8192, 4096], P('ctx', 'head'), may hold values from -6 to 6
- keys: bfloat16 [8192, 4096], P('ctx', 'head'), may hold values from -6 to 6
- values: bfloat16 [8192, 4096], P('ctx', 'head'), may hold values from -24 to 24
- upstream: bfloat16 [8192, 4096], P('ctx', 'head'), may hold values from -12 to 12
- out_weight: bfloat16 [4096, 4096], P('head'), may hold values from -0.09375 to 0.09375
Outputs:
- attention: bfloat16 [8192, 4096], P('ctx', 'head')
- grad_queries: bfloat16 [8192, 4096], P('ctx', 'head')
- grad_keys: bfloat16 [8192, 4096], P('ctx', 'head')
- grad_values: bfloat16 [8192, 4096], P('ctx', 'head')
- wo_grad: float32 [4096, 4096], P('ctx', 'head')
All inputs are finite; a program needn't handle non-finite values.
Results may differ from a plain program's by a relative error of at most 0.023.
Values may be sent and summed in bfloat16 or wider, within the bound.
A program may use at most 128 MiB of HBM per device.

v0:
```python
import math

import jax
import jax.numpy as jnp
from jax import lax
from jax.sharding import PartitionSpec as P

HDIM = 128
BLK = 256
LEVELS = 5


def from_behind(block, axis, distance):
    devices = range(lax.axis_size(axis))
    route = [(i - distance, i) for i in devices if i - distance in devices]
    return lax.ppermute(block, axis, route)


def per_device(queries, keys, values, upstream, out_weight):
    features = queries.shape[1]
    head_count = features // HDIM
    block_count = queries.shape[0] // BLK
    scaling = 1.0 / math.sqrt(HDIM)
    distances = [2**level for level in range(LEVELS)]
    device_spans = sorted(
        set((distance // block_count for distance in distances if distance >= block_count))
    )

    def to_blocks(tensor):
        return tensor.reshape(block_count, BLK, head_count, HDIM)

    own_keys = to_blocks(keys)
    own_values = to_blocks(values)
    fetched = {}
    for device_span in device_spans:
        arrived = from_behind((keys, values), "ctx", device_span)
        fetched[device_span] = (to_blocks(arrived[0]), to_blocks(arrived[1]))
    key_layers = [own_keys]
    value_layers = [own_values]
    for build_distance in distances:
        if build_distance >= block_count:
            far_keys, far_values = fetched[build_distance // block_count]
        else:
            near_keys, near_values = fetched[1]
            far_keys = jnp.concatenate([near_keys, own_keys], 0)[
                block_count - build_distance : 2 * block_count - build_distance
            ]
            far_values = jnp.concatenate([near_values, own_values], 0)[
                block_count - build_distance : 2 * block_count - build_distance
            ]
        key_layers.append(far_keys)
        value_layers.append(far_values)
    key_stack = jnp.stack(key_layers)
    value_stack = jnp.stack(value_layers)
    position = lax.axis_index("ctx")
    block_ids = position * block_count + jnp.arange(block_count)
    valid = jnp.stack([block_ids >= 0] + [block_ids >= distance for distance in distances], 1)
    row_ids = jnp.arange(BLK)
    causal = row_ids[:, None] >= row_ids[None, :]
    within = jnp.concatenate([causal[None], jnp.ones((LEVELS, BLK, BLK), jnp.bool_)], 0)
    visible = valid[:, None, :, None, None] & within[None, None]
    query_blocks = to_blocks(queries)
    scores = (
        jnp.einsum("mqhd,lmkhd->mhlqk", query_blocks, key_stack, preferred_element_type=jnp.float32)
        * scaling
    )
    row_max = jnp.max(jnp.where(visible, scores, -jnp.inf), axis=(2, 4))
    weights = jnp.where(visible, jnp.exp(scores - row_max[:, :, None, :, None]), 0.0)
    totals = jnp.sum(weights, axis=(2, 4))
    mixed = jnp.einsum(
        "mhlqk,lmkhd->mqhd",
        weights.astype(jnp.bfloat16),
        value_stack,
        preferred_element_type=jnp.float32,
    )
    attention_blocks = (mixed / jnp.transpose(totals, (0, 2, 1))[..., None]).astype(jnp.bfloat16)
    attention = attention_blocks.reshape(queries.shape)
    full_upstream = lax.all_gather(upstream, "head", axis=1, tiled=True)
    context_grad = lax.dot_general(
        full_upstream, out_weight, (((1,), (1,)), ((), ())), preferred_element_type=jnp.float32
    ).astype(jnp.bfloat16)
    row_share = out_weight.shape[1] // lax.axis_size("ctx")
    columns = lax.slice_in_dim(full_upstream, 0, row_share * lax.axis_size("ctx"), axis=1)
    wo_grad = lax.psum_scatter(
        lax.dot_general(
            columns, attention, (((0,), (0,)), ((), ())), preferred_element_type=jnp.float32
        ).astype(jnp.bfloat16),
        "ctx",
        scatter_dimension=0,
        tiled=True,
    ).astype(jnp.float32)
    grad_key_stack, grad_value_stack = (key_stack, value_stack)
    context_blocks = to_blocks(context_grad)
    normed = weights / totals[:, :, None, :, None]
    row_dots = jnp.sum(
        context_blocks.astype(jnp.float32) * attention_blocks.astype(jnp.float32), -1
    )
    row_dots = jnp.transpose(row_dots, (0, 2, 1))
    value_grads = jnp.einsum(
        "mhlqk,mqhd->lmkhd",
        normed.astype(jnp.bfloat16),
        context_blocks,
        preferred_element_type=jnp.float32,
    )
    prob_grad = jnp.einsum(
        "mqhd,lmkhd->mhlqk", context_blocks, grad_value_stack, preferred_element_type=jnp.float32
    )
    score_grad = (normed * (prob_grad - row_dots[:, :, None, :, None])).astype(jnp.bfloat16)
    query_grad = scaling * jnp.einsum(
        "mhlqk,lmkhd->mqhd", score_grad, grad_key_stack, preferred_element_type=jnp.float32
    )
    grad_queries = query_grad.reshape(queries.shape).astype(jnp.bfloat16)
    key_grads = scaling * jnp.einsum(
        "mhlqk,mqhd->lmkhd", score_grad, query_blocks, preferred_element_type=jnp.float32
    )
    local_keys = key_grads[0]
    local_values = value_grads[0]
    empty_terms = jnp.zeros(local_keys.shape, jnp.float32)
    outgoing = {}
    for device_span in device_spans:
        outgoing[device_span] = [empty_terms, empty_terms]
    for level_index, distance in enumerate(distances):
        term_keys = key_grads[level_index + 1]
        term_values = value_grads[level_index + 1]
        if distance >= block_count:
            target = outgoing[distance // block_count]
            target[0] = target[0] + term_keys
            target[1] = target[1] + term_values
        else:
            front_pad = jnp.zeros((block_count - distance,) + term_keys.shape[1:], jnp.float32)
            back_pad = jnp.zeros((distance,) + term_keys.shape[1:], jnp.float32)
            wide_keys = jnp.concatenate([front_pad, term_keys, back_pad], 0)
            wide_values = jnp.concatenate([front_pad, term_values, back_pad], 0)
            outgoing[1][0] = outgoing[1][0] + wide_keys[:block_count]
            outgoing[1][1] = outgoing[1][1] + wide_values[:block_count]
            local_keys = local_keys + wide_keys[block_count:]
            local_values = local_values + wide_values[block_count:]
    flat_shape = queries.shape
    for device_span in device_spans:
        outgoing[device_span] = [
            outgoing[device_span][0].reshape(flat_shape),
            outgoing[device_span][1].reshape(flat_shape),
        ]
    local_keys = local_keys.reshape(flat_shape)
    local_values = local_values.reshape(flat_shape)
    for device_span in device_spans:
        send_keys, send_values = outgoing[device_span]
        back_keys, back_values = from_behind((send_keys, send_values), "ctx", -device_span)
        local_keys = local_keys + back_keys
        local_values = local_values + back_values
    grad_keys = local_keys.astype(jnp.bfloat16)
    grad_values = local_values.astype(jnp.bfloat16)
    return (attention, grad_queries, grad_keys, grad_values, wo_grad)


def solution(mesh):
    placed = (
        P("ctx", "head"),
        P("ctx", "head"),
        P("ctx", "head"),
        P("ctx", "head"),
        P("head", None),
    )
    return jax.shard_map(
        per_device,
        mesh=mesh,
        in_specs=placed,
        out_specs=(
            P("ctx", "head"),
            P("ctx", "head"),
            P("ctx", "head"),
            P("ctx", "head"),
            P("ctx", "head"),
        ),
        check_vma=False,
    )
```

profile of v0, /device:TPU:4, one launch (start us, length us, event | category | flops | bytes accessed | tf_op | source)
XLA Modules:
  0.0 397.9 jit_solution(14511551288291311100)
XLA Ops:
  9.0 3.8 collective-permute-start.5
  12.9 5.2 %collective-permute-start.6 = (bf16[256,512]{0,1:T(8,128)(2,1)S(1)}, bf16[256,512]{0,1:T(8,128)(2,1)S(1)}, u32[]{:S(2)}, u32[]{:S(2)}) collective-permute-start(bf16[256,512]{0,1:T(8,128)(2,1)S(1)} %copy.92), channel_id=1, source_target_pairs={{0,16},{8,24},{16,32},{24,40},{32,48},{40,56},{48,64},{56,72},{64,... | collective-permute-start | bytes 786440 | tf_op jit(solution)/shard_map/ppermute | solution.py:16
  18.1 6.4 %collective-permute-start.7 = (bf16[256,512]{0,1:T(8,128)(2,1)S(1)}, bf16[256,512]{0,1:T(8,128)(2,1)S(1)}, u32[]{:S(2)}, u32[]{:S(2)}) collective-permute-start(bf16[256,512]{0,1:T(8,128)(2,1)S(1)} %copy.92), channel_id=1, source_target_pairs={{0,32},{8,40},{16,48},{24,56},{32,64},{40,72},{48,80},{56,88},{64,... | collective-permute-start | bytes 786440 | tf_op jit(solution)/shard_map/ppermute | solution.py:16
  24.5 3.1 collective-permute-start.8
  32.8 4.5 %collective-permute-done.6 = bf16[256,512]{0,1:T(8,128)(2,1)S(1)} collective-permute-done((bf16[256,512]{0,1:T(8,128)(2,1)S(1)}, bf16[256,512]{0,1:T(8,128)(2,1)S(1)}, u32[]{:S(2)}, u32[]{:S(2)}) %collective-permute-start.6) | collective-permute-done | bytes 262176 | tf_op jit(solution)/shard_map/ppermute | solution.py:16
  37.4 3.8 collective-permute-start.1
  41.2 6.4 %collective-permute-start.2 = (bf16[256,512]{1,0:T(8,128)(2,1)}, bf16[256,512]{1,0:T(8,128)(2,1)}, u32[]{:S(2)}, u32[]{:S(2)}) collective-permute-start(bf16[256,512]{1,0:T(8,128)(2,1)} %param.7), channel_id=1, source_target_pairs={{0,32},{8,40},{16,48},{24,56},{32,64},{40,72},{48,80},{56,88},{64,... | collective-permute-start | bytes 786440 | tf_op jit(solution)/shard_map/ppermute | solution.py:16
  47.6 3.2 collective-permute-start.3
  50.8 3.3 collective-permute-done.9
  62.5 8.5 %collective-permute-done.1 = bf16[256,512]{1,0:T(8,128)(2,1)} collective-permute-done((bf16[256,512]{1,0:T(8,128)(2,1)}, bf16[256,512]{1,0:T(8,128)(2,1)}, u32[]{:S(2)}, u32[]{:S(2)}) %collective-permute-start.1) | collective-permute-done | bytes 262176 | tf_op jit(solution)/shard_map/ppermute | solution.py:16
  84.3 2.6 copy-done
  88.3 4.2 %convolution_convert_fusion.1 = bf16[256,512]{1,0:T(8,128)(2,1)S(1)} fusion(bf16[256,4096]{1,0:T(8,128)(2,1)} %all-gather.2.cloned.1.call-done, bf16[512,4096]{1,0:T(8,128)(2,1)} %param.9), kind=kOutput, calls=%fused_computation.32 | convolution fusion | flops 1073872896 | bytes 6553600 | tf_op jit(solution)/shard_map/dot_general | solution.py:79
  92.7 4.5 %multiply_reduce_fusion = (f32[256,4]{0,1:T(4,128)S(1)}, bf16[1,256,4,128]{1,3,2,0:T(8,128)(2,1)S(1)}) fusion(f32[1,256,4,128]{1,3,2,0:T(8,128)S(1)} %bitcast.207, f32[256,4]{0,1:T(4,128)S(1)} %bitcast.211, f32[4,6,256,256]{3,2,1,0:T(8,128)} %copy-done, f32[4,256]{1,0:T(4,128)S(1)} %get-tuple-element.32, pred[6,256,256]{1,2,0:T(8,128)(4,1)S(1)} %pad_and_fusion, ...), kind=kOutput, calls=%fused_computation.38 | convolution fusion | flops 409598976 | bytes 9056256 | tf_op jit(solution)/shard_map/mhlqk,lmkhd->mqhd/dot_general | solution.py:70
  97.8 3.3 fusion.4
  101.1 6.6 %copy.150 = bf16[4096,512]{1,0:T(8,128)(2,1)} copy(bf16[4096,512]{0,1:T(8,128)(2,1)} %fusion.4) | data formatting | bytes 8388608
  108.7 5.8 %fusion.9 = bf16[4,6,256,256]{2,3,1,0:T(8,128)(2,1)S(1)} fusion(f32[4,256]{1,0:T(4,128)S(1)} %bitcast.213, f32[4,256]{1,0:T(4,128)S(1)} %fusion.6, f32[4,256]{1,0:T(4,128)S(1)} %get-tuple-element.32, f32[4,6,256,256]{3,2,1,0:T(8,128)} %copy-done, pred[6,256,256]{1,2,0:T(8,128)(4,1)S(1)} %pad_and_fusion, bf16[256,4,128,1]{0,2,3,1:T(8,128)(2,1)} %copy.140, ...), kind=kOutput, calls=%fused_computation.14 | convolution fusion | flops 413663232 | bytes 11677696 | tf_op jit(solution)/shard_map/mqhd,lmkhd->mhlqk/dot_general | solution.py:105
  119.4 2.1 collective-permute-start.14
  123.6 3.1 collective-permute-start.13
  128.7 2.9 collective-permute-start.12
  133.7 7.4 %collective-permute-start.11 = (f32[256,512]{1,0:T(8,128)}, f32[256,512]{1,0:T(8,128)}, u32[]{:S(2)}, u32[]{:S(2)}) collective-permute-start(f32[256,512]{1,0:T(8,128)} %copy.115), channel_id=1, source_target_pairs={{16,0},{24,8},{32,16},{40,24},{48,32},{56,40},{64,48},{72,56},{80,... | collective-permute-start | bytes 1572872 | tf_op jit(solution)/shard_map/ppermute | solution.py:16
  145.0 6.7 %fusion.17 = f32[6,1,256,4,128]{2,4,0,3,1:T(8,128)} fusion(bf16[256,4,128,1]{0,2,3,1:T(8,128)(2,1)} %copy.140, f32[4,256]{1,0:T(4,128)S(1)} %fusion.6, f32[4,256]{1,0:T(4,128)S(1)} %get-tuple-element.32, f32[4,6,256,256]{3,2,1,0:T(8,128)} %copy-done, pred[6,256,256]{1,2,0:T(8,128)(4,1)S(1)} %pad_and_fusion), kind=kOutput, calls=%fused_computation.21 | convolution fusion | flops 410517504 | bytes 10100736 | tf_op jit(solution)/shard_map/mhlqk,mqhd->lmkhd/dot_general | solution.py:99
  153.5 3.6 fusion.54
  171.4 5.5 %collective-permute-start.17 = (f32[256,512]{1,0:T(8,128)}, f32[256,512]{1,0:T(8,128)}, u32[]{:S(2)}, u32[]{:S(2)}) collective-permute-start(f32[256,512]{1,0:T(8,128)} %copy.124), channel_id=1, source_target_pairs={{32,0},{40,8},{48,16},{56,24},{64,32},{72,40},{80,48},{88,56},{96,... | collective-permute-start | bytes 1572872 | tf_op jit(solution)/shard_map/ppermute | solution.py:16
  176.9 9.0 %collective-permute-done.11 = f32[256,512]{1,0:T(8,128)} collective-permute-done((f32[256,512]{1,0:T(8,128)}, f32[256,512]{1,0:T(8,128)}, u32[]{:S(2)}, u32[]{:S(2)}) %collective-permute-start.11) | collective-permute-done | bytes 524320 | tf_op jit(solution)/shard_map/ppermute | solution.py:16
  185.9 10.4 %collective-permute-start.16 = (f32[256,512]{1,0:T(8,128)}, f32[256,512]{1,0:T(8,128)}, u32[]{:S(2)}, u32[]{:S(2)}) collective-permute-start(f32[256,512]{1,0:T(8,128)} %copy.123), channel_id=1, source_target_pairs={{16,0},{24,8},{32,16},{40,24},{48,32},{56,40},{64,48},{72,56},{80,... | collective-permute-start | bytes 1572872 | tf_op jit(solution)/shard_map/ppermute | solution.py:16
  196.3 37.3 %collective-permute-done.10 = f32[256,512]{1,0:T(8,128)} collective-permute-done((f32[256,512]{1,0:T(8,128)}, f32[256,512]{1,0:T(8,128)}, u32[]{:S(2)}, u32[]{:S(2)}) %collective-permute-start.10) | collective-permute-done | bytes 524320 | tf_op jit(solution)/shard_map/ppermute | solution.py:16
  233.6 7.0 %collective-permute-start.15 = (f32[256,512]{1,0:T(8,128)}, f32[256,512]{1,0:T(8,128)}, u32[]{:S(2)}, u32[]{:S(2)}) collective-permute-start(f32[256,512]{1,0:T(8,128)} %copy.121), channel_id=1, source_target_pairs={{8,0},{16,8},{24,16},{32,24},{40,32},{48,40},{56,48},{64,56},{72,6... | collective-permute-start | bytes 1572872 | tf_op jit(solution)/shard_map/ppermute | solution.py:16
  240.6 2.2 fusion.37
  246.1 2.7 add_convert_fusion.1
  249.2 13.3 %collective-permute-done.15 = f32[256,512]{1,0:T(8,128)} collective-permute-done((f32[256,512]{1,0:T(8,128)}, f32[256,512]{1,0:T(8,128)}, u32[]{:S(2)}, u32[]{:S(2)}) %collective-permute-start.15) | collective-permute-done | bytes 524320 | tf_op jit(solution)/shard_map/ppermute | solution.py:16
  262.6 2.7 add_convert_fusion
  265.2 124.0 %reduce-scatter.4.cloned.1.call-done = bf16[128,512]{1,0:T(8,128)(2,1)} async-done(((bf16[4096,512]{1,0:T(8,128)(2,1)}), bf16[128,512]{1,0:T(8,128)(2,1)}) %reduce-scatter.4.cloned.1.call-update) | async-done | bytes 131088
  (105 shorter events, 68.4 us)
Async XLA Ops:
  7.2 48.3 %copy-start.10 = (bf16[256,512]{1,0:T(8,128)(2,1)S(1)}, bf16[256,512]{1,0:T(8,128)(2,1)}, u32[]{:S(2)}) copy-start(bf16[256,512]{1,0:T(8,128)(2,1)} %param.5) | copy-start | bytes 786436
  7.2 81.1 %all-gather.2.cloned.1.call-start = ((), (), s32[]{:S(2)}) async-start(), calls=%async_computation.1 | async-start | bytes 2359296 | tf_op jit(solution)/shard_map/all_gather | solution.py:78
  7.9 381.3 %reduce-scatter.4.cloned.1.call-start = ((), (), s32[]{:S(2)}) async-start(), calls=%async_computation.2 | async-start | bytes 4325376
  9.0 21.9 %collective-permute-start.5 = (bf16[256,512]{0,1:T(8,128)(2,1)S(1)}, bf16[256,512]{0,1:T(8,128)(2,1)S(1)}, u32[]{:S(2)}, u32[]{:S(2)}) collective-permute-start(bf16[256,512]{0,1:T(8,128)(2,1)S(1)} %copy.92), channel_id=1, source_target_pairs={{0,8},{8,16},{16,24},{24,32},{32,40},{40,48},{48,56},{56,64},{64,7... | collective-permute-start | bytes 786440 | tf_op jit(solution)/shard_map/ppermute | solution.py:16
  12.9 24.5 %collective-permute-start.6 = (bf16[256,512]{0,1:T(8,128)(2,1)S(1)}, bf16[256,512]{0,1:T(8,128)(2,1)S(1)}, u32[]{:S(2)}, u32[]{:S(2)}) collective-permute-start(bf16[256,512]{0,1:T(8,128)(2,1)S(1)} %copy.92), channel_id=1, source_target_pairs={{0,16},{8,24},{16,32},{24,40},{32,48},{40,56},{48,64},{56,72},{64,... | collective-permute-start | bytes 786440 | tf_op jit(solution)/shard_map/ppermute | solution.py:16
  18.1 23.1 %collective-permute-start.7 = (bf16[256,512]{0,1:T(8,128)(2,1)S(1)}, bf16[256,512]{0,1:T(8,128)(2,1)S(1)}, u32[]{:S(2)}, u32[]{:S(2)}) collective-permute-start(bf16[256,512]{0,1:T(8,128)(2,1)S(1)} %copy.92), channel_id=1, source_target_pairs={{0,32},{8,40},{16,48},{24,56},{32,64},{40,72},{48,80},{56,88},{64,... | collective-permute-start | bytes 786440 | tf_op jit(solution)/shard_map/ppermute | solution.py:16
  24.5 23.1 %collective-permute-start.8 = (bf16[256,512]{0,1:T(8,128)(2,1)S(1)}, bf16[256,512]{0,1:T(8,128)(2,1)}, u32[]{:S(2)}, u32[]{:S(2)}) collective-permute-start(bf16[256,512]{0,1:T(8,128)(2,1)S(1)} %copy.92), channel_id=1, source_target_pairs={{0,64},{8,72},{16,80},{24,88},{32,96},{40,104},{48,112},{56,120},{... | collective-permute-start | bytes 786440 | tf_op jit(solution)/shard_map/ppermute | solution.py:16
  27.6 26.5 %collective-permute-start.9 = (bf16[256,512]{0,1:T(8,128)(2,1)S(1)}, bf16[256,512]{0,1:T(8,128)(2,1)}, u32[]{:S(2)}, u32[]{:S(2)}) collective-permute-start(bf16[256,512]{0,1:T(8,128)(2,1)S(1)} %copy.92), channel_id=1, source_target_pairs={{0,128},{8,136},{16,144},{24,152},{32,160},{40,168},{48,176},{56,1... | collective-permute-start | bytes 786440 | tf_op jit(solution)/shard_map/ppermute | solution.py:16
  30.9 30.5 %collective-permute-start = (bf16[256,512]{1,0:T(8,128)(2,1)}, bf16[256,512]{1,0:T(8,128)(2,1)}, u32[]{:S(2)}, u32[]{:S(2)}) collective-permute-start(bf16[256,512]{1,0:T(8,128)(2,1)} %param.7), channel_id=1, source_target_pairs={{0,8},{8,16},{16,24},{24,32},{32,40},{40,48},{48,56},{56,64},{64,7... | collective-permute-start | bytes 786440 | tf_op jit(solution)/shard_map/ppermute | solution.py:16
  37.4 18.7 %copy-start.11 = (bf16[256,512]{0,1:T(8,128)(2,1)}, bf16[256,512]{0,1:T(8,128)(2,1)S(1)}, u32[]{:S(2)}) copy-start(bf16[256,512]{0,1:T(8,128)(2,1)S(1)} %collective-permute-done.6) | copy-start | bytes 786436
  37.4 33.6 %collective-permute-start.1 = (bf16[256,512]{1,0:T(8,128)(2,1)}, bf16[256,512]{1,0:T(8,128)(2,1)}, u32[]{:S(2)}, u32[]{:S(2)}) collective-permute-start(bf16[256,512]{1,0:T(8,128)(2,1)} %param.7), channel_id=1, source_target_pairs={{0,16},{8,24},{16,32},{24,40},{32,48},{40,56},{48,64},{56,72},{64,... | collective-permute-start | bytes 786440 | tf_op jit(solution)/shard_map/ppermute | solution.py:16
  41.2 14.6 %copy-start.12 = (bf16[256,512]{0,1:T(8,128)(2,1)}, bf16[256,512]{0,1:T(8,128)(2,1)S(1)}, u32[]{:S(2)}) copy-start(bf16[256,512]{0,1:T(8,128)(2,1)S(1)} %collective-permute-done.7) | copy-start | bytes 786436
  41.2 31.6 %collective-permute-start.2 = (bf16[256,512]{1,0:T(8,128)(2,1)}, bf16[256,512]{1,0:T(8,128)(2,1)}, u32[]{:S(2)}, u32[]{:S(2)}) collective-permute-start(bf16[256,512]{1,0:T(8,128)(2,1)} %param.7), channel_id=1, source_target_pairs={{0,32},{8,40},{16,48},{24,56},{32,64},{40,72},{48,80},{56,88},{64,... | collective-permute-start | bytes 786440 | tf_op jit(solution)/shard_map/ppermute | solution.py:16
  47.6 27.0 %collective-permute-start.3 = (bf16[256,512]{1,0:T(8,128)(2,1)}, bf16[256,512]{1,0:T(8,128)(2,1)}, u32[]{:S(2)}, u32[]{:S(2)}) collective-permute-start(bf16[256,512]{1,0:T(8,128)(2,1)} %param.7), channel_id=1, source_target_pairs={{0,64},{8,72},{16,80},{24,88},{32,96},{40,104},{48,112},{56,120},{... | collective-permute-start | bytes 786440 | tf_op jit(solution)/shard_map/ppermute | solution.py:16
  54.1 22.3 %collective-permute-start.4 = (bf16[256,512]{1,0:T(8,128)(2,1)}, bf16[256,512]{1,0:T(8,128)(2,1)}, u32[]{:S(2)}, u32[]{:S(2)}) collective-permute-start(bf16[256,512]{1,0:T(8,128)(2,1)} %param.7), channel_id=1, source_target_pairs={{0,128},{8,136},{16,144},{24,152},{32,160},{40,168},{48,176},{56,1... | collective-permute-start | bytes 786440 | tf_op jit(solution)/shard_map/ppermute | solution.py:16
  55.7 27.5 %copy-start.3 = (bf16[256,4,128,1]{0,2,3,1:T(8,128)(2,1)}, bf16[256,4,128,1]{0,2,3,1:T(8,128)(2,1)S(1)}, u32[]{:S(2)}) copy-start(bf16[256,4,128,1]{0,2,3,1:T(8,128)(2,1)S(1)} %copy.139) | copy-start | bytes 786436
  78.2 3.6 copy-start.8
  78.2 4.3 %copy-start.9 = (bf16[256,512]{0,1:T(8,128)(2,1)S(1)}, bf16[256,512]{0,1:T(8,128)(2,1)}, u32[]{:S(2)}) copy-start(bf16[256,512]{0,1:T(8,128)(2,1)} %copy.91) | copy-start | bytes 786436
  79.4 4.8 %copy-start.1 = (bf16[6,1,256,4,128]{4,2,0,3,1:T(8,128)(2,1)}, bf16[6,1,256,4,128]{4,2,0,3,1:T(8,128)(2,1)S(1)}, u32[]{:S(2)}) copy-start(bf16[6,1,256,4,128]{4,2,0,3,1:T(8,128)(2,1)S(1)} %constant_dynamic-update-slice_fusion.6) | copy-start | bytes 4718596
  88.2 4.4 %copy-start.13 = (bf16[6,1,256,4,128]{2,4,0,3,1:T(8,128)(2,1)S(1)}, bf16[6,1,256,4,128]{2,4,0,3,1:T(8,128)(2,1)}, u32[]{:S(2)}) copy-start(bf16[6,1,256,4,128]{2,4,0,3,1:T(8,128)(2,1)} %constant_dynamic-update-slice_fusion) | copy-start | bytes 4718596
  92.7 5.2 %copy-start.2 = (bf16[256,4096]{1,0:T(8,128)(2,1)S(1)}, bf16[256,4096]{1,0:T(8,128)(2,1)}, u32[]{:S(2)}) copy-start(bf16[256,4096]{1,0:T(8,128)(2,1)} %all-gather.2.cloned.1.call-done) | copy-start | bytes 6291460
  108.7 5.8 %copy-start.4 = (bf16[256,4,128,1]{0,2,3,1:T(8,128)(2,1)S(1)}, bf16[256,4,128,1]{0,2,3,1:T(8,128)(2,1)}, u32[]{:S(2)}) copy-start(bf16[256,4,128,1]{0,2,3,1:T(8,128)(2,1)} %copy-done.3) | copy-start | bytes 786436
  119.4 48.0 %collective-permute-start.14 = (f32[256,512]{1,0:T(8,128)}, f32[256,512]{1,0:T(8,128)}, u32[]{:S(2)}, u32[]{:S(2)}) collective-permute-start(f32[256,512]{1,0:T(8,128)} %copy.118), channel_id=1, source_target_pairs={{128,0},{136,8},{144,16},{152,24},{160,32},{168,40},{176,48},{184,... | collective-permute-start | bytes 1572872 | tf_op jit(solution)/shard_map/ppermute | solution.py:16
  123.6 45.9 %collective-permute-start.13 = (f32[256,512]{1,0:T(8,128)}, f32[256,512]{1,0:T(8,128)}, u32[]{:S(2)}, u32[]{:S(2)}) collective-permute-start(f32[256,512]{1,0:T(8,128)} %copy.117), channel_id=1, source_target_pairs={{64,0},{72,8},{80,16},{88,24},{96,32},{104,40},{112,48},{120,56},{... | collective-permute-start | bytes 1572872 | tf_op jit(solution)/shard_map/ppermute | solution.py:16
  128.7 42.7 %collective-permute-start.12 = (f32[256,512]{1,0:T(8,128)}, f32[256,512]{1,0:T(8,128)}, u32[]{:S(2)}, u32[]{:S(2)}) collective-permute-start(f32[256,512]{1,0:T(8,128)} %copy.116), channel_id=1, source_target_pairs={{32,0},{40,8},{48,16},{56,24},{64,32},{72,40},{80,48},{88,56},{96,... | collective-permute-start | bytes 1572872 | tf_op jit(solution)/shard_map/ppermute | solution.py:16
  133.7 52.3 %collective-permute-start.11 = (f32[256,512]{1,0:T(8,128)}, f32[256,512]{1,0:T(8,128)}, u32[]{:S(2)}, u32[]{:S(2)}) collective-permute-start(f32[256,512]{1,0:T(8,128)} %copy.115), channel_id=1, source_target_pairs={{16,0},{24,8},{32,16},{40,24},{48,32},{56,40},{64,48},{72,56},{80,... | collective-permute-start | bytes 1572872 | tf_op jit(solution)/shard_map/ppermute | solution.py:16
  143.1 90.5 %collective-permute-start.10 = (f32[256,512]{1,0:T(8,128)}, f32[256,512]{1,0:T(8,128)}, u32[]{:S(2)}, u32[]{:S(2)}) collective-permute-start(f32[256,512]{1,0:T(8,128)} %copy.113), channel_id=1, source_target_pairs={{8,0},{16,8},{24,16},{32,24},{40,32},{48,40},{56,48},{64,56},{72,6... | collective-permute-start | bytes 1572872 | tf_op jit(solution)/shard_map/ppermute | solution.py:16
  167.4 81.4 %collective-permute-start.19 = (f32[256,512]{1,0:T(8,128)}, f32[256,512]{1,0:T(8,128)}, u32[]{:S(2)}, u32[]{:S(2)}) collective-permute-start(f32[256,512]{1,0:T(8,128)} %copy.126), channel_id=1, source_target_pairs={{128,0},{136,8},{144,16},{152,24},{160,32},{168,40},{176,48},{184,... | collective-permute-start | bytes 1572872 | tf_op jit(solution)/shard_map/ppermute | solution.py:16
  169.4 79.3 %collective-permute-start.18 = (f32[256,512]{1,0:T(8,128)}, f32[256,512]{1,0:T(8,128)}, u32[]{:S(2)}, u32[]{:S(2)}) collective-permute-start(f32[256,512]{1,0:T(8,128)} %copy.125), channel_id=1, source_target_pairs={{64,0},{72,8},{80,16},{88,24},{96,32},{104,40},{112,48},{120,56},{... | collective-permute-start | bytes 1572872 | tf_op jit(solution)/shard_map/ppermute | solution.py:16
  171.4 77.4 %collective-permute-start.17 = (f32[256,512]{1,0:T(8,128)}, f32[256,512]{1,0:T(8,128)}, u32[]{:S(2)}, u32[]{:S(2)}) collective-permute-start(f32[256,512]{1,0:T(8,128)} %copy.124), channel_id=1, source_target_pairs={{32,0},{40,8},{48,16},{56,24},{64,32},{72,40},{80,48},{88,56},{96,... | collective-permute-start | bytes 1572872 | tf_op jit(solution)/shard_map/ppermute | solution.py:16
  185.9 63.3 %collective-permute-start.16 = (f32[256,512]{1,0:T(8,128)}, f32[256,512]{1,0:T(8,128)}, u32[]{:S(2)}, u32[]{:S(2)}) collective-permute-start(f32[256,512]{1,0:T(8,128)} %copy.123), channel_id=1, source_target_pairs={{16,0},{24,8},{32,16},{40,24},{48,32},{56,40},{64,48},{72,56},{80,... | collective-permute-start | bytes 1572872 | tf_op jit(solution)/shard_map/ppermute | solution.py:16
  233.6 28.9 %collective-permute-start.15 = (f32[256,512]{1,0:T(8,128)}, f32[256,512]{1,0:T(8,128)}, u32[]{:S(2)}, u32[]{:S(2)}) collective-permute-start(f32[256,512]{1,0:T(8,128)} %copy.121), channel_id=1, source_target_pairs={{8,0},{16,8},{24,16},{32,24},{40,32},{48,40},{56,48},{64,56},{72,6... | collective-permute-start | bytes 1572872 | tf_op jit(solution)/shard_map/ppermute | solution.py:16
  (4 other events, 8.2 us)
Sparse Core Ops, SparseCore 0:
  9.8 30.6 all-gather.1
  107.9 281.2 reduce-scatter.3
where the time goes:
time: 401 us; the launch traced here: 398 us
  waiting for transfers between devices  201 us (50%)
  starting transfers between devices  80.7 us (20%)
  local copies, waits for them, and re-layouts  65.7 us (16%)
  matrix products  28.8 us (7%)
  between operations  14.6 us (4%)
  other arithmetic  6.92 us (2%)
    unnamed x3, waiting for transfers between devices  125 us
    ppermute x20, starting transfers between devices, from_behind(): return lax.ppermute(block, axis, route)  80.6 us
    ppermute x20, waiting for transfers between devices, from_behind(): return lax.ppermute(block, axis, route)  76.5 us
    unnamed x45, local copies, waits for them, and re-layouts  21.5 us
    another operation x5, local copies, waits for them, and re-layouts, per_device(): outgoing[device_span][1].reshape(flat_shape)  10.3 us
    another operation x5, local copies, waits for them, and re-layouts, per_device(): outgoing[device_span][0].reshape(flat_shape)  10.2 us
    ppermute x5, local copies, waits for them, and re-layouts, from_behind(): return lax.ppermute(block, axis, route)  8.24 us
  transfers between devices with their start and end apart: 22, of which 8 were waited for; matrix products, arithmetic and copies ran while one was open for 19% of the time, Pallas kernels for 0%

commit v1 on v0

v1 whole, which is shorter than its diff:
```python
import functools
import math

import jax
import jax.numpy as jnp
from jax import lax
from jax.experimental import pallas as pl
from jax.experimental.pallas import tpu as pltpu
from jax.sharding import PartitionSpec as P

HDIM = 128
BLK = 256
DISTANCES = (0, 1, 2, 4, 8, 16)
LV = len(DISTANCES)
HEADS = 4
FEAT = HEADS * HDIM
D = 4096
CTX = 32
ZS = 8
XS = 4
HP = 8
SCALING = 1.0 / math.sqrt(HDIM)
MESH = pl.DeviceIdType.MESH
BF16 = jnp.bfloat16
F32 = jnp.float32

KV_ROUTE = {1: (0, 1), 2: (1, 1), 3: (2, 2), 4: (0, 8), 5: (4, 8)}


def wrap(i, n):
    return lax.rem(i + n, n)


def dot_nt(a, b):
    return lax.dot_general(a, b, (((1,), (1,)), ((), ())), preferred_element_type=F32)


def dot_nn(a, b):
    return lax.dot_general(a, b, (((1,), (0,)), ((), ())), preferred_element_type=F32)


def dot_tn(a, b):
    return lax.dot_general(a, b, (((0,), (0,)), ((), ())), preferred_element_type=F32)


def kernel(
    q_in, k_in, v_in, up_in, w_in,
    att_o, dq_o, dk_o, dv_o, wo_o,
    kv, qh, fu, wv, uu, cg_acc, cgh, sc, nb, att_all, own, gs, gr, wos, wor,
    loc, kv_s, kv_r, gr_s, gr_r, fu_s, fu_r, ua_s, ua_r, ug_s, ug_r, at_s, at_r, wo_s, wo_r,
):
    c = lax.axis_index("ctx")
    h = lax.axis_index("head")
    x = lax.div(c, ZS)
    z = lax.rem(c, ZS)
    owns = lax.rem(c, XS) == x

    def at_ctx(shift):
        return (lax.rem(c + (shift + CTX), CTX), h)

    def at_head(shift):
        return (c, lax.rem(h + shift, HP))

    def cols(j, width):
        return pl.ds(pl.multiple_of(j * width, 128), width)

    def local_copy(i):
        kind, j = divmod(i, HEADS)
        src = (k_in, v_in, q_in)[kind].at[:, j * HDIM : (j + 1) * HDIM]
        dst = qh.at[j] if kind == 2 else kv.at[j, kind, 0]
        return pltpu.make_async_copy(src, dst, loc.at[i])

    up_copy = pltpu.make_async_copy(up_in, fu.at[h], loc.at[12])
    piece_copy = pltpu.make_async_copy(up_in.at[:, cols(x, HDIM)], uu.at[h, x], loc.at[13])
    w_copy = pltpu.make_async_copy(w_in, wv, loc.at[14])

    def kv_copy(lv, j):
        src, shift = KV_ROUTE[lv]
        return pltpu.make_async_remote_copy(
            kv.at[j, :, src], kv.at[j, :, lv], kv_s.at[lv - 1, j], kv_r.at[lv - 1, j],
            device_id=at_ctx(shift), device_id_type=MESH)

    def gr_copy(lv, j):
        shift = KV_ROUTE[lv][1]
        return pltpu.make_async_remote_copy(
            gs.at[lv - 1, j], gr.at[lv - 1, j], gr_s.at[lv - 1, j], gr_r.at[lv - 1, j],
            device_id=at_ctx(-shift), device_id_type=MESH)

    def fu_copy(s):
        return pltpu.make_async_remote_copy(
            up_in, fu.at[h], fu_s.at[s], fu_r.at[s], device_id=at_head(s), device_id_type=MESH)

    def ua_copy(s):
        target = lax.rem(x + s, XS)
        return pltpu.make_async_remote_copy(
            up_in.at[:, cols(target, HDIM)], uu.at[h, x], ua_s.at[s], ua_r.at[s],
            device_id=at_ctx(s * ZS), device_id_type=MESH)

    def ug_copy(s):
        return pltpu.make_async_remote_copy(
            uu.at[h], uu.at[h], ug_s.at[s], ug_r.at[s], device_id=at_head(s), device_id_type=MESH)

    def at_copy(s, j):
        part = att_all.at[x, :, cols(j, HDIM)]
        return pltpu.make_async_remote_copy(
            part, part, at_s.at[s, j], at_r.at[s, j], device_id=at_ctx(s * ZS), device_id_type=MESH)

    def wo_copy(i):
        return pltpu.make_async_remote_copy(
            wos.at[i], wor.at[z], wo_s.at[i], wo_r.at[z], device_id=(XS * i + x, h),
            device_id_type=MESH)

    def wo_arrival(i):
        return pltpu.make_async_remote_copy(
            wos.at[i], wor.at[i], wo_s.at[i], wo_r.at[i], device_id=(XS * i + x, h),
            device_id_type=MESH)

    for i in range(12):
        local_copy(i).start()
    up_copy.start()
    piece_copy.start()
    w_copy.start()

    barrier = pltpu.get_barrier_semaphore()
    for shift in (1, 2, -1, -2, 8, 16, 24):
        pl.semaphore_signal(barrier, inc=1, device_id=at_ctx(shift), device_id_type=MESH)
    for s in range(1, HP):
        pl.semaphore_signal(barrier, inc=1, device_id=at_head(s), device_id_type=MESH)

    def greet(i, carry):
        sender = ZS * lax.rem(c, XS) + i

        @pl.when(sender != c)
        def _():
            pl.semaphore_signal(barrier, inc=1, device_id=(sender, h), device_id_type=MESH)

        return carry

    lax.fori_loop(0, ZS, greet, 0)

    @pl.when(owns)
    def _():
        pl.semaphore_wait(barrier, 21)

    @pl.when(jnp.logical_not(owns))
    def _():
        pl.semaphore_wait(barrier, 22)

    for j in range(HEADS):
        local_copy(j).wait()
        local_copy(HEADS + j).wait()
        kv_copy(1, j).start()
        kv_copy(4, j).start()
    for s in range(1, XS):
        ua_copy(s).start()
    for s in range(1, HP):
        fu_copy(s).start()

    def relay_one(j, carry):
        kv_copy(1, j).wait_recv()
        kv_copy(2, j).start()
        kv_copy(4, j).wait_recv()
        kv_copy(5, j).start()
        return carry

    lax.fori_loop(0, HEADS, relay_one, 0)
    piece_copy.wait()
    for s in range(1, XS):
        ua_copy(s).wait_recv()
    for s in range(1, HP):
        ug_copy(s).start()

    def relay_two(j, carry):
        kv_copy(2, j).wait_recv()
        kv_copy(3, j).start()
        return carry

    lax.fori_loop(0, HEADS, relay_two, 0)

    w_copy.wait()
    up_copy.wait()
    cg_acc[...] = dot_nt(fu[h], wv[:, cols(h, FEAT)])

    def context_step(s, carry):
        fu_copy(s).wait_recv()
        peer = lax.rem(h + (HP - s), HP)
        cg_acc[...] += dot_nt(fu[peer], wv[:, cols(peer, FEAT)])
        return carry

    lax.fori_loop(1, HP, context_step, 0)
    for j in range(HEADS):
        cgh[j] = cg_acc[:, j * HDIM : (j + 1) * HDIM].astype(BF16)
        local_copy(2 * HEADS + j).wait()

    def head(j):
        kv_copy(3, j).wait_recv()
        kv_copy(5, j).wait_recv()
        q = qh[j]
        cg = cgh[j]
        row_max = None
        for lv in range(LV):
            s = dot_nt(kv[j, 0, lv], q) * SCALING
            if lv == 0:
                key_id = lax.broadcasted_iota(jnp.int32, (BLK, BLK), 0)
                query_id = lax.broadcasted_iota(jnp.int32, (BLK, BLK), 1)
                s = jnp.where(key_id <= query_id, s, -1e30)
            else:
                s = s + jnp.where(c >= DISTANCES[lv], 0.0, -1e30).astype(F32)
            sc[lv] = s
            top = jnp.max(s, axis=0, keepdims=True)
            row_max = top if row_max is None else jnp.maximum(row_max, top)
        totals = jnp.zeros((1, BLK), F32)
        for lv in range(LV):
            w = jnp.exp(sc[lv] - row_max)
            sc[lv] = w
            totals = totals + jnp.sum(w, axis=0, keepdims=True)
            nb[lv * BLK : (lv + 1) * BLK, :] = w.astype(BF16)
        inverse = 1.0 / totals
        mixed = dot_tn(kv[j, 1].reshape(LV * BLK, HDIM), nb[...])
        att_t = (mixed * inverse).astype(BF16).astype(F32)
        att = att_t.T.astype(BF16)
        att_o[:, cols(j, HDIM)] = att
        att_all[x, :, cols(j, HDIM)] = att
        for s in range(1, XS):
            at_copy(s, j).start()
        row_dots = jnp.sum(cg.astype(F32).T * att_t, axis=0, keepdims=True)
        for lv in range(LV):
            normed = sc[lv] * inverse
            prob_grad = dot_nt(kv[j, 1, lv], cg)
            ds = (normed * (prob_grad - row_dots)).astype(BF16)
            nb[lv * BLK : (lv + 1) * BLK, :] = ds
            dv = dot_nn(normed.astype(BF16), cg)
            dk = dot_nn(ds, q) * SCALING
            if lv in (3, 5):
                gs[lv - 1, j, 0] = dk.astype(BF16)
                gs[lv - 1, j, 1] = dv.astype(BF16)
                gr_copy(lv, j).start()
            else:
                own[lv, j, 0] = dk
                own[lv, j, 1] = dv
        dq_t = dot_tn(kv[j, 0].reshape(LV * BLK, HDIM), nb[...]) * SCALING
        dq_o[:, cols(j, HDIM)] = dq_t.T.astype(BF16)

    def pass_on(src, dst, j):
        gr_copy(src, j).wait_recv()
        gs[dst - 1, j] = (own[dst, j] + gr[src - 1, j].astype(F32)).astype(BF16)
        gr_copy(dst, j).start()

    def stage(t, do_head):
        if do_head:
            head(t)

        @pl.when((t >= 1) & (t < HEADS + 1))
        def _():
            pass_on(3, 2, t - 1)
            pass_on(5, 4, t - 1)

        @pl.when((t >= 2) & (t < HEADS + 2))
        def _():
            pass_on(2, 1, t - 2)

        @pl.when(t >= 3)
        def _():
            j = t - 3
            gr_copy(1, j).wait_recv()
            gr_copy(4, j).wait_recv()
            total = own[0, j] + gr[0, j].astype(F32) + gr[3, j].astype(F32)
            dk_o[:, cols(j, HDIM)] = total[0].astype(BF16)
            dv_o[:, cols(j, HDIM)] = total[1].astype(BF16)

    def stage_head(t, carry):
        stage(t, True)
        return carry

    def stage_tail(t, carry):
        stage(t, False)
        return carry

    lax.fori_loop(0, HEADS, stage_head, 0)

    for s in range(1, XS):
        for j in range(HEADS):
            at_copy(s, j).wait_recv()
    for s in range(1, HP):
        ug_copy(s).wait_recv()

    def project(n, carry):
        i = lax.rem(z + n, HP)
        part = dot_tn(
            uu[i].reshape(XS * BLK, HDIM), att_all[...].reshape(XS * BLK, FEAT)
        ).astype(BF16)

        @pl.when(XS * i + x != c)
        def _():
            wos[i] = part
            wo_copy(i).start()

        @pl.when(XS * i + x == c)
        def _():
            wor[z] = part

        return carry

    lax.fori_loop(0, HP, project, 0)

    lax.fori_loop(HEADS, HEADS + 3, stage_tail, 0)

    wo_o[...] = jnp.zeros((HDIM, FEAT), F32)

    def gather(i, carry):
        @pl.when(ZS * lax.rem(c, XS) + i != c)
        def _():
            wo_arrival(i).wait_recv()

        wo_o[...] += wor[i].astype(F32)
        return carry

    lax.fori_loop(0, ZS, gather, 0)

    def drain(j, carry):
        for lv in range(1, LV):
            kv_copy(lv, j).wait_send()
            gr_copy(lv, j).wait_send()
        for s in range(1, XS):
            at_copy(s, j).wait_send()
        return carry

    lax.fori_loop(0, HEADS, drain, 0)
    for s in range(1, XS):
        ua_copy(s).wait_send()
    for s in range(1, HP):
        fu_copy(s).wait_send()
        ug_copy(s).wait_send()

    def drain_wo(i, carry):
        @pl.when(XS * i + x != c)
        def _():
            wo_copy(i).wait_send()

        return carry

    lax.fori_loop(0, HP, drain_wo, 0)


def per_device(queries, keys, values, upstream, out_weight):
    tokens = jax.ShapeDtypeStruct((BLK, FEAT), BF16)
    dma = pltpu.SemaphoreType.DMA
    vmem = pltpu.VMEM
    return pl.pallas_call(
        kernel,
        out_shape=(tokens, tokens, tokens, tokens, jax.ShapeDtypeStruct((HDIM, FEAT), F32)),
        in_specs=[pl.BlockSpec(memory_space=pl.ANY)] * 5,
        out_specs=(pl.BlockSpec(memory_space=pltpu.VMEM),) * 5,
        scratch_shapes=[
            vmem((HEADS, 2, LV, BLK, HDIM), BF16),
            vmem((HEADS, BLK, HDIM), BF16),
            vmem((HP, BLK, FEAT), BF16),
            vmem((FEAT, D), BF16),
            vmem((HP, XS, BLK, HDIM), BF16),
            vmem((BLK, FEAT), F32),
            vmem((HEADS, BLK, HDIM), BF16),
            vmem((LV, BLK, BLK), F32),
            vmem((LV * BLK, BLK), BF16),
            vmem((XS, BLK, FEAT), BF16),
            vmem((5, HEADS, 2, BLK, HDIM), F32),
            vmem((5, HEADS, 2, BLK, HDIM), BF16),
            vmem((5, HEADS, 2, BLK, HDIM), BF16),
            vmem((HP, HDIM, FEAT), BF16),
            vmem((ZS, HDIM, FEAT), BF16),
            dma((15,)),
            dma((5, HEADS)), dma((5, HEADS)),
            dma((5, HEADS)), dma((5, HEADS)),
            dma((HP,)), dma((HP,)),
            dma((XS,)), dma((XS,)),
            dma((HP,)), dma((HP,)),
            dma((XS, HEADS)), dma((XS, HEADS)),
            dma((HP,)), dma((ZS,)),
        ],
        compiler_params=pltpu.CompilerParams(
            collective_id=0, has_side_effects=True, vmem_limit_bytes=56 * 1024 * 1024
        ),
        cost_estimate=pl.CostEstimate(flops=5 * 10**9, bytes_accessed=10**7, transcendentals=2 * 10**6),
        name="log_sparse_attention",
    )(queries, keys, values, upstream, out_weight)


def solution(mesh):
    tiled = P("ctx", "head")
    return jax.shard_map(
        per_device,
        mesh=mesh,
        in_specs=(tiled, tiled, tiled, tiled, P("head", None)),
        out_specs=(tiled,) * 5,
        check_vma=False,
    )
```

time: 401 us -> 187 us (0.47)
  the two profiles are of different devices: /device:TPU:4 before, /device:TPU:204 now
where the time goes in v1:
time: 187 us
  Pallas kernels  178 us (95%)
  local copies, waits for them, and re-layouts  8.35 us (4%)
    pallas_call x1, Pallas kernels, per_device(): pl.pallas_call(kernel, out_shape=(tokens, tokens, tokens, tokens, jax.Sha...  178 us
    unnamed x5, local copies, waits for them, and re-layouts  8.35 us

profile of v1, /device:TPU:204, one launch (start us, length us, event | category | flops | bytes accessed | tf_op | source)
XLA Modules:
  0.0 187.1 jit_solution(212904092463905800)
XLA Ops:
  0.6 178.2 %log_sparse_attention.1 = (bf16[256,512]{1,0:T(8,128)(2,1)}, bf16[256,512]{1,0:T(8,128)(2,1)}, bf16[256,512]{1,0:T(8,128)(2,1)}, bf16[256,512]{1,0:T(8,128)(2,1)}, f32[128,512]{1,0:T(8,128)}) custom-call(bf16[256,512]{1,0:T(8,128)(2,1)} %q_in.1, bf16[256,512]{1,0:T(8,128)(2,1)} %k_in.1, bf16[256,512]{1,0:T(8,128)(2,1)} %v_in.1, bf16[256,512]{1,0:T(8,128)(2,1)} %up_in.1, ...), custom_call_target="tpu_custom_call" | custom-call | flops 5000000000 | bytes 10000000 | tf_op jit(solution)/shard_map/log_sparse_attention/pallas_call | solution.py:349
  178.8 1.7 copy.15
  180.5 1.7 copy.16
  182.1 1.7 copy.17
  183.8 1.7 copy.18
  185.5 1.7 copy.19

commit v2 on v1

v2 whole, which is shorter than its diff:
```python
import math

import jax
import jax.numpy as jnp
from jax import lax
from jax.experimental import pallas as pl
from jax.experimental.pallas import tpu as pltpu
from jax.sharding import PartitionSpec as P

HDIM = 128
BLK = 256
DISTANCES = (0, 1, 2, 4, 8, 16)
LV = len(DISTANCES)
HEADS = 4
FEAT = HEADS * HDIM
D = 4096
CTX = 32
ZS = 8
XS = 4
HP = 8
SCALING = 1.0 / math.sqrt(HDIM)
MESH = pl.DeviceIdType.MESH
BF16 = jnp.bfloat16
F32 = jnp.float32

KV_ROUTE = {1: (0, 1), 2: (1, 1), 3: (2, 2), 4: (0, 8), 5: (4, 8)}


def dot_nt(a, b):
    return lax.dot_general(a, b, (((1,), (1,)), ((), ())), preferred_element_type=F32)


def dot_nn(a, b):
    return lax.dot_general(a, b, (((1,), (0,)), ((), ())), preferred_element_type=F32)


def dot_tn(a, b):
    return lax.dot_general(a, b, (((0,), (0,)), ((), ())), preferred_element_type=F32)


def kernel(
    q_in, k_in, v_in, up_in, w_in,
    att_o, dq_o, dk_o, dv_o, wo_o,
    kv, qh, fu, wv, ust, uu, cg_acc, cgh, sc, nb, att_all, own, gs, gr, wos, wor,
    loc, kv_s, kv_r, gr_s, gr_r, fy_s, fy_r, fc_s, fc_r, ua_s, ua_r, uy_s, uy_r, uc_s, uc_r,
    at_s, at_r, wo_s, wo_r,
):
    c = lax.axis_index("ctx")
    h = lax.axis_index("head")
    x = lax.div(c, ZS)
    z = lax.rem(c, ZS)
    core = lax.rem(h, 2)
    twin = h + 1 - 2 * core

    def at_ctx(shift):
        return (lax.rem(c + (shift + CTX), CTX), h)

    def at_z(shift):
        return (x * ZS + lax.rem(z + (shift + ZS), ZS), h)

    def at_head(shift):
        return (c, lax.rem(h + shift, HP))

    def cols(j, width):
        return pl.ds(pl.multiple_of(j * width, 128), width)

    def remote(src, dst, send, recv, device):
        return pltpu.make_async_remote_copy(
            src, dst, send, recv, device_id=device, device_id_type=MESH)

    def local_copy(kind, j):
        src = (k_in, v_in, q_in)[kind].at[:, j * HDIM : (j + 1) * HDIM]
        dst = qh.at[j] if kind == 2 else kv.at[j, kind, 0]
        return pltpu.make_async_copy(src, dst, loc.at[kind * HEADS + j])

    up_copy = pltpu.make_async_copy(up_in, fu.at[h], loc.at[12])
    w_copy = pltpu.make_async_copy(w_in, wv, loc.at[13])

    def kv_copy(lv, j, src=None):
        route, shift = KV_ROUTE[lv]
        return remote(
            kv.at[j, :, route if src is None else src], kv.at[j, :, lv],
            kv_s.at[lv - 1, j], kv_r.at[lv - 1, j], at_z(1) if lv == 1 else at_ctx(shift))

    def gr_copy(lv, j):
        return remote(
            gs.at[lv - 1, j], gr.at[lv - 1, j], gr_s.at[lv - 1, j], gr_r.at[lv - 1, j],
            at_ctx(-KV_ROUTE[lv][1]))

    def from_y(s):
        return lax.rem(h + (HP - 2 * s), HP)

    def fy_copy(s):
        return remote(up_in, fu.at[h], fy_s.at[s], fy_r.at[s], at_head(2 * s))

    def fc_copy(s):
        slot = from_y(s)
        return remote(up_in if s == 0 else fu.at[slot], fu.at[slot], fc_s.at[s], fc_r.at[s], (c, twin))

    def ua_copy(s):
        return remote(ust.at[s], uu.at[h, x], ua_s.at[s], ua_r.at[s], at_ctx(s * ZS))

    def uy_copy(s):
        return remote(uu.at[h], uu.at[h], uy_s.at[s], uy_r.at[s], at_head(2 * s))

    def uc_copy(s):
        slot = from_y(s)
        return remote(uu.at[slot], uu.at[slot], uc_s.at[s], uc_r.at[s], (c, twin))

    def at_copy(s, j):
        part = att_all.at[x, j]
        return remote(part, part, at_s.at[s, j], at_r.at[s, j], at_ctx(s * ZS))

    def wo_copy(n, j):
        return remote(wos.at[n, j], wor.at[z, j], wo_s.at[n, j], wo_r.at[n, j], at_z(n))

    for j in range(HEADS):
        local_copy(0, j).start()
        local_copy(1, j).start()
    up_copy.start()
    for j in range(HEADS):
        local_copy(2, j).start()
    w_copy.start()

    barrier = pltpu.get_barrier_semaphore()
    peers = [at_ctx(shift) for shift in (1, -1, 2, -2, 8, 16, 24)]
    peers += [at_head(s) for s in (2, 4, 6)] + [(c, twin)]
    peers += [at_z(s) for s in range(1, ZS)]
    for peer in peers:
        pl.semaphore_signal(barrier, inc=1, device_id=peer, device_id_type=MESH)
    pl.semaphore_wait(barrier, len(peers))

    for j in range(HEADS):
        local_copy(0, j).wait()
        local_copy(1, j).wait()
        if j < 2:
            @pl.when(z < ZS - 1)
            def _():
                kv_copy(1, j).start()
        kv_copy(4, j).start()
        if j == 0:
            fc_copy(0).start()
            for s in range(1, XS):
                fy_copy(s).start()

    def relay(j):
        kv_copy(4, j).wait_recv()
        kv_copy(5, j).start()

        @pl.when(z == ZS - 1)
        def _():
            kv_copy(1, j, 4).start()

        kv_copy(1, j).wait_recv()
        kv_copy(2, j).start()

        @pl.when((j < HEADS - 2) & (z < ZS - 1))
        def _():
            kv_copy(1, j + 2).start()

        kv_copy(2, j).wait_recv()
        kv_copy(3, j).start()

    def context():
        for s in range(1, XS):
            fy_copy(s).wait_recv()
            fc_copy(s).start()
        w_copy.wait()
        up_copy.wait()
        cg_acc[...] = dot_nt(fu[h], wv[:, cols(h, FEAT)])

        def add_tile(tile):
            cg_acc[...] += dot_nt(fu[tile], wv[:, cols(tile, FEAT)])

        def near(s, carry):
            add_tile(lax.rem(h + (HP - 2 * s), HP))
            return carry

        lax.fori_loop(1, XS, near, 0)
        for s in range(XS):
            fc_copy(s).wait_recv()

        def twins(s, carry):
            add_tile(lax.rem(twin + (HP - 2 * s), HP))
            return carry

        lax.fori_loop(0, XS, twins, 0)
        for j in range(HEADS):
            cgh[j] = cg_acc[:, j * HDIM : (j + 1) * HDIM].astype(BF16)
            local_copy(2, j).wait()
        for s in range(XS):
            target = lax.rem(x + s, XS)
            tile = fu[2 * target + lax.div(h, 4), :, cols(lax.rem(h, 4), HDIM)].T
            if s == 0:
                uu[h, x] = tile
            else:
                ust[s] = tile
                ua_copy(s).start()

    def spread_columns():
        for s in range(1, XS):
            ua_copy(s).wait_recv()
        uc_copy(0).start()
        for s in range(1, XS):
            uy_copy(s).start()

    def finish_columns():
        for s in range(1, XS):
            uy_copy(s).wait_recv()
            uc_copy(s).start()
        for s in range(XS):
            uc_copy(s).wait_recv()

    def head(j):
        kv_copy(3, j).wait_recv()
        kv_copy(5, j).wait_recv()
        q = qh[j]
        cg = cgh[j]
        row_max = None
        for lv in range(LV):
            s = dot_nt(kv[j, 0, lv], q) * SCALING
            if lv == 0:
                key_id = lax.broadcasted_iota(jnp.int32, (BLK, BLK), 0)
                query_id = lax.broadcasted_iota(jnp.int32, (BLK, BLK), 1)
                s = jnp.where(key_id <= query_id, s, -1e30)
            else:
                s = s + jnp.where(c >= DISTANCES[lv], 0.0, -1e30).astype(F32)
            sc[lv] = s
            top = jnp.max(s, axis=0, keepdims=True)
            row_max = top if row_max is None else jnp.maximum(row_max, top)
        totals = jnp.zeros((1, BLK), F32)
        for lv in range(LV):
            w = jnp.exp(sc[lv] - row_max)
            sc[lv] = w
            totals = totals + jnp.sum(w, axis=0, keepdims=True)
            nb[lv * BLK : (lv + 1) * BLK, :] = w.astype(BF16)
        inverse = 1.0 / totals
        mixed = dot_tn(kv[j, 1].reshape(LV * BLK, HDIM), nb[...])
        att_t = (mixed * inverse).astype(BF16).astype(F32)
        att = att_t.T.astype(BF16)
        att_o[:, cols(j, HDIM)] = att
        att_all[x, j] = att
        for s in range(1, XS):
            at_copy(s, j).start()
        row_dots = jnp.sum(cg.astype(F32).T * att_t, axis=0, keepdims=True)
        for lv in range(LV):
            normed = sc[lv] * inverse
            prob_grad = dot_nt(kv[j, 1, lv], cg)
            ds = (normed * (prob_grad - row_dots)).astype(BF16)
            nb[lv * BLK : (lv + 1) * BLK, :] = ds
            dv = dot_nn(normed.astype(BF16), cg)
            dk = dot_nn(ds, q) * SCALING
            if lv in (3, 5):
                gs[lv - 1, j, 0] = dk.astype(BF16)
                gs[lv - 1, j, 1] = dv.astype(BF16)
                gr_copy(lv, j).start()
            else:
                own[lv, j, 0] = dk
                own[lv, j, 1] = dv
        dq_t = dot_tn(kv[j, 0].reshape(LV * BLK, HDIM), nb[...]) * SCALING
        dq_o[:, cols(j, HDIM)] = dq_t.T.astype(BF16)

    def pass_on(src, dst, j):
        gr_copy(src, j).wait_recv()
        gs[dst - 1, j] = (own[dst, j] + gr[src - 1, j].astype(F32)).astype(BF16)
        gr_copy(dst, j).start()

    def chain_one(j):
        pass_on(3, 2, j)
        pass_on(5, 4, j)

    def chain_two(j):
        pass_on(2, 1, j)

    def last(j):
        gr_copy(1, j).wait_recv()
        gr_copy(4, j).wait_recv()
        total = own[0, j] + gr[0, j].astype(F32) + gr[3, j].astype(F32)
        dk_o[:, cols(j, HDIM)] = total[0].astype(BF16)
        dv_o[:, cols(j, HDIM)] = total[1].astype(BF16)

    def project(j):
        for s in range(1, XS):
            at_copy(s, j).wait_recv()

        def piece(n):
            i = lax.rem(z + n, ZS)
            part = dot_nn(uu[i, 0], att_all[0, j])
            for row in range(1, XS):
                part = part + dot_nn(uu[i, row], att_all[row, j])
            return part.astype(BF16)

        def send(n, carry):
            wos[n, j] = piece(n)
            wo_copy(n, j).start()
            return carry

        lax.fori_loop(1, ZS, send, 0)
        wor[z, j] = piece(0)

    def stage(t, carry):
        @pl.when(t < HEADS)
        def _():
            relay(t)

        @pl.when(t == 1)
        def _():
            context()

        @pl.when(t >= 1)
        def _():
            head(t - 1)

        @pl.when(t == 1)
        def _():
            spread_columns()

        @pl.when(t == 3)
        def _():
            finish_columns()

        @pl.when(t >= 3)
        def _():
            project(t - 3)

        @pl.when(t >= 2)
        def _():
            chain_one(t - 2)

        @pl.when(t >= 3)
        def _():
            chain_two(t - 3)

        return carry

    lax.fori_loop(0, HEADS + 1, stage, 0)
    project(2)
    project(3)
    chain_one(3)
    chain_two(2)
    last(0)
    last(1)
    chain_two(3)
    last(2)
    last(3)

    def gather(j, carry):
        for n in range(1, ZS):
            wo_copy(n, j).wait_recv()
        total = wor[0, j].astype(F32)
        for n in range(1, ZS):
            total = total + wor[n, j].astype(F32)
        wo_o[:, cols(j, HDIM)] = total
        return carry

    lax.fori_loop(0, HEADS, gather, 0)

    def drain(j, carry):
        for lv in range(1, LV):
            kv_copy(lv, j).wait_send()
            gr_copy(lv, j).wait_send()
        for s in range(1, XS):
            at_copy(s, j).wait_send()
        for n in range(1, ZS):
            wo_copy(n, j).wait_send()
        return carry

    lax.fori_loop(0, HEADS, drain, 0)
    fc_copy(0).wait_send()
    uc_copy(0).wait_send()
    for s in range(1, XS):
        fy_copy(s).wait_send()
        fc_copy(s).wait_send()
        ua_copy(s).wait_send()
        uy_copy(s).wait_send()
        uc_copy(s).wait_send()


def hand_over(*refs):
    copies = [pltpu.make_async_copy(refs[i], refs[5 + i], refs[10].at[i]) for i in range(5)]
    for copy in copies:
        copy.start()
    for copy in copies:
        copy.wait()


def per_device(queries, keys, values, upstream, out_weight):
    tokens = jax.ShapeDtypeStruct((BLK, FEAT), BF16)
    shapes = (tokens, tokens, tokens, tokens, jax.ShapeDtypeStruct((HDIM, FEAT), F32))
    dma = pltpu.SemaphoreType.DMA
    vmem = pltpu.VMEM
    results = pl.pallas_call(
        kernel,
        out_shape=shapes,
        in_specs=[pl.BlockSpec(memory_space=pl.ANY)] * 5,
        out_specs=(pl.BlockSpec(memory_space=pltpu.VMEM),) * 5,
        scratch_shapes=[
            vmem((HEADS, 2, LV, BLK, HDIM), BF16),
            vmem((HEADS, BLK, HDIM), BF16),
            vmem((HP, BLK, FEAT), BF16),
            vmem((FEAT, D), BF16),
            vmem((XS, HDIM, BLK), BF16),
            vmem((HP, XS, HDIM, BLK), BF16),
            vmem((BLK, FEAT), F32),
            vmem((HEADS, BLK, HDIM), BF16),
            vmem((LV, BLK, BLK), F32),
            vmem((LV * BLK, BLK), BF16),
            vmem((XS, HEADS, BLK, HDIM), BF16),
            vmem((5, HEADS, 2, BLK, HDIM), F32),
            vmem((5, HEADS, 2, BLK, HDIM), BF16),
            vmem((5, HEADS, 2, BLK, HDIM), BF16),
            vmem((ZS, HEADS, HDIM, HDIM), BF16),
            vmem((ZS, HEADS, HDIM, HDIM), BF16),
            dma((14,)),
            dma((5, HEADS)), dma((5, HEADS)),
            dma((5, HEADS)), dma((5, HEADS)),
            dma((XS,)), dma((XS,)), dma((XS,)), dma((XS,)),
            dma((XS,)), dma((XS,)),
            dma((XS,)), dma((XS,)), dma((XS,)), dma((XS,)),
            dma((XS, HEADS)), dma((XS, HEADS)),
            dma((ZS, HEADS)), dma((ZS, HEADS)),
        ],
        compiler_params=pltpu.CompilerParams(
            collective_id=0, has_side_effects=True, vmem_limit_bytes=52 * 1024 * 1024
        ),
        cost_estimate=pl.CostEstimate(flops=5 * 10**9, bytes_accessed=10**7, transcendentals=2 * 10**6),
        name="log_sparse_attention",
    )(queries, keys, values, upstream, out_weight)
    return pl.pallas_call(
        hand_over,
        out_shape=shapes,
        in_specs=[pl.BlockSpec(memory_space=pltpu.VMEM)] * 5,
        out_specs=(pl.BlockSpec(memory_space=pl.ANY),) * 5,
        scratch_shapes=[dma((5,))],
        compiler_params=pltpu.CompilerParams(vmem_limit_bytes=4 * 1024 * 1024),
        name="hand_over",
    )(*results)


def solution(mesh):
    tiled = P("ctx", "head")
    return jax.shard_map(
        per_device,
        mesh=mesh,
        in_specs=(tiled, tiled, tiled, tiled, P("head", None)),
        out_specs=(tiled,) * 5,
        check_vma=False,
    )
```

time: 187 us -> 124 us (0.66)
  the two profiles are of different devices: /device:TPU:204 before, /device:TPU:4 now
where the time goes in v2:
time: 124 us; the launch traced here: 122 us
  Pallas kernels  120 us (97%)
  local copies, waits for them, and re-layouts  1.89 us (2%)
    pallas_call x1, Pallas kernels, per_device(): pl.pallas_call(kernel, out_shape=shapes, in_specs=[pl.BlockSpec(memory_sp...  119 us

profile of v2, /device:TPU:4, one launch (start us, length us, event | category | flops | bytes accessed | tf_op | source)
XLA Modules:
  0.0 122.3 jit_solution(11522861645625361537)
XLA Ops:
  0.6 0.0 copy-start
  0.6 0.9 copy-done
  1.6 0.0 copy-start.1
  1.6 0.9 copy-done.1
  2.5 118.6 %log_sparse_attention.1 = (bf16[256,512]{1,0:T(8,128)(2,1)S(1)}, bf16[256,512]{1,0:T(8,128)(2,1)S(1)}, bf16[256,512]{1,0:T(8,128)(2,1)S(1)}, bf16[256,512]{1,0:T(8,128)(2,1)S(1)}, f32[128,512]{1,0:T(8,128)S(1)}) custom-call(bf16[256,512]{1,0:T(8,128)(2,1)S(1)} %copy-done, bf16[256,512]{1,0:T(8,128)(2,1)S(1)} %copy-done.1, bf16[256,512]{1,0:T(8,128)(2,1)} %v_in.1, ...), custom_call_target="tpu_custom_call" | custom-call | flops 5000000000 | bytes 10000000 | tf_op jit(solution)/shard_map/log_sparse_attention/pallas_call | solution.py:392
  121.2 1.1 hand_over.1
Async XLA Ops:
  0.6 1.0 copy-start
  1.6 0.9 copy-start.1

commit v3 on v2

--- a/solution.py
+++ b/solution.py
@@ -17,6 +17,10 @@
 CTX = 32
 ZS = 8
 XS = 4
+UP = 4
+DOWN = 3
+GROUPS = 2
+WIDE = FEAT // GROUPS
 HP = 8
 SCALING = 1.0 / math.sqrt(HDIM)
 MESH = pl.DeviceIdType.MESH
@@ -41,8 +45,8 @@
 def kernel(
     q_in, k_in, v_in, up_in, w_in,
     att_o, dq_o, dk_o, dv_o, wo_o,
-    kv, qh, fu, wv, ust, uu, cg_acc, cgh, sc, nb, att_all, own, gs, gr, wos, wor,
-    loc, kv_s, kv_r, gr_s, gr_r, fy_s, fy_r, fc_s, fc_r, ua_s, ua_r, uy_s, uy_r, uc_s, uc_r,
+    kv, held, qh, fu, wv, ust, uu, cg_acc, cgh, sc, nb, att_all, own, gs, gr, held_gr, part, wos, wor,
+    loc, kv_s, kv_r, nk_s, nk_r, gr_s, gr_r, gn_s, gn_r, fy_s, fy_r, fc_s, fc_r, ua_s, ua_r, uy_s, uy_r, uc_s, uc_r,
     at_s, at_r, wo_s, wo_r,
 ):
     c = lax.axis_index("ctx")
@@ -87,6 +91,18 @@
             gs.at[lv - 1, j], gr.at[lv - 1, j], gr_s.at[lv - 1, j], gr_r.at[lv - 1, j],
             at_ctx(-KV_ROUTE[lv][1]))
 
+    def nk_copy(j, src):
+        return remote(kv.at[j, :, src], held.at[j], nk_s.at[j], nk_r.at[j], at_z(-2))
+
+    def nk_relay(j):
+        return remote(held.at[j], kv.at[j, :, 3], kv_s.at[2, j], kv_r.at[2, j], at_z(-2))
+
+    def gn_copy(j):
+        return remote(gs.at[2, j], held_gr.at[j - 2], gn_s.at[j - 2], gn_r.at[j - 2], at_z(2))
+
+    def gn_relay(j):
+        return remote(held_gr.at[j - 2], gr.at[2, j], gr_s.at[2, j], gr_r.at[2, j], at_z(2))
+
     def from_y(s):
         return lax.rem(h + (HP - 2 * s), HP)
 
@@ -108,11 +124,13 @@
         return remote(uu.at[slot], uu.at[slot], uc_s.at[s], uc_r.at[s], (c, twin))
 
     def at_copy(s, j):
-        part = att_all.at[x, j]
-        return remote(part, part, at_s.at[s, j], at_r.at[s, j], at_ctx(s * ZS))
-
-    def wo_copy(n, j):
-        return remote(wos.at[n, j], wor.at[z, j], wo_s.at[n, j], wo_r.at[n, j], at_z(n))
+        piece = att_all.at[x, lax.div(j, 2), :, cols(lax.rem(j, 2), HDIM)]
+        return remote(piece, piece, at_s.at[s, j], at_r.at[s, j], at_ctx(s * ZS))
+
+    def wo_copy(g, way, k):
+        return remote(
+            wos.at[g, way, k], wor.at[g, way, k], wo_s.at[g, way, k], wo_r.at[g, way, k],
+            at_z(1 - 2 * way))
 
     for j in range(HEADS):
         local_copy(0, j).start()
@@ -125,7 +143,7 @@
     barrier = pltpu.get_barrier_semaphore()
     peers = [at_ctx(shift) for shift in (1, -1, 2, -2, 8, 16, 24)]
     peers += [at_head(s) for s in (2, 4, 6)] + [(c, twin)]
-    peers += [at_z(s) for s in range(1, ZS)]
+    peers += [at_z(s) for s in (1, -1, 2, -2)]
     for peer in peers:
         pl.semaphore_signal(barrier, inc=1, device_id=peer, device_id_type=MESH)
     pl.semaphore_wait(barrier, len(peers))
@@ -137,13 +155,18 @@
             @pl.when(z < ZS - 1)
             def _():
                 kv_copy(1, j).start()
+
+            @pl.when(z < ZS // 2)
+            def _():
+                nk_copy(j, 0).start()
+
         kv_copy(4, j).start()
         if j == 0:
             fc_copy(0).start()
             for s in range(1, XS):
                 fy_copy(s).start()
 
-    def relay(j):
+    def relay_near(j):
         kv_copy(4, j).wait_recv()
         kv_copy(5, j).start()
 
@@ -151,43 +174,36 @@
         def _():
             kv_copy(1, j, 4).start()
 
+        if j < 2:
+            @pl.when(z >= ZS // 2)
+            def _():
+                nk_copy(j, 4).start()
+
         kv_copy(1, j).wait_recv()
         kv_copy(2, j).start()
 
-        @pl.when((j < HEADS - 2) & (z < ZS - 1))
-        def _():
-            kv_copy(1, j + 2).start()
-
+        if j < 2:
+            @pl.when(z < ZS - 1)
+            def _():
+                kv_copy(1, j + 2).start()
+
+    def relay_down(j):
+        nk_copy(j, 0).wait_recv()
+        nk_relay(j).start()
+
+    def relay_up(j):
         kv_copy(2, j).wait_recv()
         kv_copy(3, j).start()
 
-    def context():
+    def pass_upstream():
         for s in range(1, XS):
             fy_copy(s).wait_recv()
             fc_copy(s).start()
-        w_copy.wait()
-        up_copy.wait()
-        cg_acc[...] = dot_nt(fu[h], wv[:, cols(h, FEAT)])
-
-        def add_tile(tile):
-            cg_acc[...] += dot_nt(fu[tile], wv[:, cols(tile, FEAT)])
-
-        def near(s, carry):
-            add_tile(lax.rem(h + (HP - 2 * s), HP))
-            return carry
-
-        lax.fori_loop(1, XS, near, 0)
+
+    def exchange_columns():
         for s in range(XS):
             fc_copy(s).wait_recv()
-
-        def twins(s, carry):
-            add_tile(lax.rem(twin + (HP - 2 * s), HP))
-            return carry
-
-        lax.fori_loop(0, XS, twins, 0)
-        for j in range(HEADS):
-            cgh[j] = cg_acc[:, j * HDIM : (j + 1) * HDIM].astype(BF16)
-            local_copy(2, j).wait()
+        up_copy.wait()
         for s in range(XS):
             target = lax.rem(x + s, XS)
             tile = fu[2 * target + lax.div(h, 4), :, cols(lax.rem(h, 4), HDIM)].T
@@ -197,6 +213,19 @@
                 ust[s] = tile
                 ua_copy(s).start()
 
+    def context():
+        w_copy.wait()
+        cg_acc[...] = dot_nt(fu[0], wv[:, 0:FEAT])
+
+        def add_tile(tile, carry):
+            cg_acc[...] += dot_nt(fu[tile], wv[:, cols(tile, FEAT)])
+            return carry
+
+        lax.fori_loop(1, HP, add_tile, 0)
+        for j in range(HEADS):
+            cgh[j] = cg_acc[:, j * HDIM : (j + 1) * HDIM].astype(BF16)
+            local_copy(2, j).wait()
+
     def spread_columns():
         for s in range(1, XS):
             ua_copy(s).wait_recv()
@@ -212,6 +241,10 @@
             uc_copy(s).wait_recv()
 
     def head(j):
+        @pl.when(j < 2)
+        def _():
+            kv_copy(2, j).wait_recv()
+
         kv_copy(3, j).wait_recv()
         kv_copy(5, j).wait_recv()
         q = qh[j]
@@ -239,7 +272,7 @@
         att_t = (mixed * inverse).astype(BF16).astype(F32)
         att = att_t.T.astype(BF16)
         att_o[:, cols(j, HDIM)] = att
-        att_all[x, j] = att
+        att_all[x, lax.div(j, 2), :, cols(lax.rem(j, 2), HDIM)] = att
         for s in range(1, XS):
             at_copy(s, j).start()
         row_dots = jnp.sum(cg.astype(F32).T * att_t, axis=0, keepdims=True)
@@ -253,10 +286,25 @@
             if lv in (3, 5):
                 gs[lv - 1, j, 0] = dk.astype(BF16)
                 gs[lv - 1, j, 1] = dv.astype(BF16)
-                gr_copy(lv, j).start()
+                if lv == 5:
+                    gr_copy(lv, j).start()
+                else:
+                    @pl.when(j < 2)
+                    def _():
+                        gr_copy(3, j).start()
+
+                    @pl.when(j >= 2)
+                    def _():
+                        gn_copy(j).start()
             else:
                 own[lv, j, 0] = dk
                 own[lv, j, 1] = dv
+                if lv == 2:
+                    @pl.when(j >= 2)
+                    def _():
+                        gs[1, j, 0] = dk.astype(BF16)
+                        gs[1, j, 1] = dv.astype(BF16)
+                        gr_copy(2, j).start()
         dq_t = dot_tn(kv[j, 0].reshape(LV * BLK, HDIM), nb[...]) * SCALING
         dq_o[:, cols(j, HDIM)] = dq_t.T.astype(BF16)
 
@@ -267,93 +315,124 @@
 
     def chain_one(j):
         pass_on(3, 2, j)
-        pass_on(5, 4, j)
 
     def chain_two(j):
         pass_on(2, 1, j)
+
+    def send_up(j):
+        gn_copy(j).wait_recv()
+        gn_relay(j).start()
+
+    upper = (z >= ZS // 2).astype(F32)
+
+    def eight(j):
+        if j < 2:
+            pass_on(5, 4, j)
+        else:
+            gr_copy(5, j).wait_recv()
+            gr_copy(3, j).wait_recv()
+            total = own[4, j] + gr[4, j].astype(F32) + upper * gr[2, j].astype(F32)
+            gs[3, j] = total.astype(BF16)
+            gr_copy(4, j).start()
 
     def last(j):
         gr_copy(1, j).wait_recv()
         gr_copy(4, j).wait_recv()
         total = own[0, j] + gr[0, j].astype(F32) + gr[3, j].astype(F32)
+        if j >= 2:
+            total = total + (1.0 - upper) * gr[2, j].astype(F32)
         dk_o[:, cols(j, HDIM)] = total[0].astype(BF16)
         dv_o[:, cols(j, HDIM)] = total[1].astype(BF16)
 
-    def project(j):
-        for s in range(1, XS):
-            at_copy(s, j).wait_recv()
-
-        def piece(n):
-            i = lax.rem(z + n, ZS)
-            part = dot_nn(uu[i, 0], att_all[0, j])
+    def project(g):
+        for j in (2 * g, 2 * g + 1):
+            for s in range(1, XS):
+                at_copy(s, j).wait_recv()
+
+        def pieces(n, carry):
+            rows = pl.ds(n * 4, 4)
+            total = dot_nn(uu[rows, 0].reshape(4 * HDIM, BLK), att_all[0, g])
             for row in range(1, XS):
-                part = part + dot_nn(uu[i, row], att_all[row, j])
-            return part.astype(BF16)
-
-        def send(n, carry):
-            wos[n, j] = piece(n)
-            wo_copy(n, j).start()
+                total = total + dot_nn(uu[rows, row].reshape(4 * HDIM, BLK), att_all[row, g])
+            part[g, rows] = total.reshape(4, HDIM, WIDE)
             return carry
 
-        lax.fori_loop(1, ZS, send, 0)
-        wor[z, j] = piece(0)
+        lax.fori_loop(0, ZS // 4, pieces, 0)
+        for way, steps in ((0, UP), (1, DOWN)):
+            wos[g, way, 0] = part[g, target_of(way, steps)].astype(BF16)
+            wo_copy(g, way, 0).start()
+
+    def target_of(way, left):
+        return lax.rem(z + (left if way == 0 else ZS - left), ZS)
+
+    def ring(g, k):
+        for way, steps in ((0, UP), (1, DOWN)):
+            if k > steps:
+                continue
+            wo_copy(g, way, k - 1).wait_recv()
+            if k < steps:
+                total = wor[g, way, k - 1].astype(F32) + part[g, target_of(way, steps - k)]
+                wos[g, way, k] = total.astype(BF16)
+                wo_copy(g, way, k).start()
+            elif way == 1:
+                part[g, z] = part[g, z] + wor[g, way, k - 1].astype(F32)
+            else:
+                wo_o[:, g * WIDE : (g + 1) * WIDE] = part[g, z] + wor[g, way, k - 1].astype(F32)
+
+    relay_near(0)
+    relay_down(0)
+    relay_near(1)
+    pass_upstream()
+    relay_down(1)
+    relay_near(2)
+    exchange_columns()
+    relay_near(3)
+    context()
+    relay_up(2)
 
     def stage(t, carry):
-        @pl.when(t < HEADS)
-        def _():
-            relay(t)
-
         @pl.when(t == 1)
         def _():
-            context()
-
-        @pl.when(t >= 1)
-        def _():
-            head(t - 1)
-
-        @pl.when(t == 1)
+            relay_up(3)
+
+        @pl.when(t == 2)
         def _():
             spread_columns()
 
         @pl.when(t == 3)
         def _():
-            finish_columns()
-
-        @pl.when(t >= 3)
-        def _():
-            project(t - 3)
-
-        @pl.when(t >= 2)
-        def _():
-            chain_one(t - 2)
-
-        @pl.when(t >= 3)
-        def _():
-            chain_two(t - 3)
-
+            chain_one(0)
+
+        head(t)
         return carry
 
-    lax.fori_loop(0, HEADS + 1, stage, 0)
-    project(2)
-    project(3)
-    chain_one(3)
+    lax.fori_loop(0, HEADS, stage, 0)
+    chain_one(1)
+    send_up(2)
+    finish_columns()
     chain_two(2)
-    last(0)
+    project(0)
+    project(1)
+    eight(1)
+    chain_two(0)
+    ring(0, 1)
+    ring(1, 1)
+    send_up(3)
+    eight(2)
+    chain_two(1)
+    ring(0, 2)
+    ring(1, 2)
+    eight(0)
     last(1)
     chain_two(3)
+    eight(3)
+    ring(0, 3)
+    ring(1, 3)
+    last(0)
     last(2)
+    ring(0, 4)
     last(3)
-
-    def gather(j, carry):
-        for n in range(1, ZS):
-            wo_copy(n, j).wait_recv()
-        total = wor[0, j].astype(F32)
-        for n in range(1, ZS):
-            total = total + wor[n, j].astype(F32)
-        wo_o[:, cols(j, HDIM)] = total
-        return carry
-
-    lax.fori_loop(0, HEADS, gather, 0)
+    ring(1, 4)
 
     def drain(j, carry):
         for lv in range(1, LV):
@@ -361,11 +440,16 @@
             gr_copy(lv, j).wait_send()
         for s in range(1, XS):
             at_copy(s, j).wait_send()
-        for n in range(1, ZS):
-            wo_copy(n, j).wait_send()
         return carry
 
     lax.fori_loop(0, HEADS, drain, 0)
+    for j in (0, 1):
+        nk_copy(j, 0).wait_send()
+        gn_copy(j + 2).wait_send()
+    for g in range(GROUPS):
+        for way, steps in ((0, UP), (1, DOWN)):
+            for k in range(steps):
+                wo_copy(g, way, k).wait_send()
     fc_copy(0).wait_send()
     uc_copy(0).wait_send()
     for s in range(1, XS):
@@ -396,6 +480,7 @@
         out_specs=(pl.BlockSpec(memory_space=pltpu.VMEM),) * 5,
         scratch_shapes=[
             vmem((HEADS, 2, LV, BLK, HDIM), BF16),
+            vmem((2, 2, BLK, HDIM), BF16),
             vmem((HEADS, BLK, HDIM), BF16),
             vmem((HP, BLK, FEAT), BF16),
             vmem((FEAT, D), BF16),
@@ -405,20 +490,24 @@
             vmem((HEADS, BLK, HDIM), BF16),
             vmem((LV, BLK, BLK), F32),
             vmem((LV * BLK, BLK), BF16),
-            vmem((XS, HEADS, BLK, HDIM), BF16),
+            vmem((XS, GROUPS, BLK, WIDE), BF16),
             vmem((5, HEADS, 2, BLK, HDIM), F32),
             vmem((5, HEADS, 2, BLK, HDIM), BF16),
             vmem((5, HEADS, 2, BLK, HDIM), BF16),
-            vmem((ZS, HEADS, HDIM, HDIM), BF16),
-            vmem((ZS, HEADS, HDIM, HDIM), BF16),
+            vmem((2, 2, BLK, HDIM), BF16),
+            vmem((GROUPS, ZS, HDIM, WIDE), F32),
+            vmem((GROUPS, 2, UP, HDIM, WIDE), BF16),
+            vmem((GROUPS, 2, UP, HDIM, WIDE), BF16),
             dma((14,)),
             dma((5, HEADS)), dma((5, HEADS)),
+            dma((2,)), dma((2,)),
             dma((5, HEADS)), dma((5, HEADS)),
+            dma((2,)), dma((2,)),
             dma((XS,)), dma((XS,)), dma((XS,)), dma((XS,)),
             dma((XS,)), dma((XS,)),
             dma((XS,)), dma((XS,)), dma((XS,)), dma((XS,)),
             dma((XS, HEADS)), dma((XS, HEADS)),
-            dma((ZS, HEADS)), dma((ZS, HEADS)),
+            dma((GROUPS, 2, UP)), dma((GROUPS, 2, UP)),
         ],
         compiler_params=pltpu.CompilerParams(
             collective_id=0, has_side_effects=True, vmem_limit_bytes=52 * 1024 * 1024

time: 124 us -> 101 us (0.81)
  Pallas kernels: 120 us -> 98 us
    pallas_call x1, Pallas kernels: 119 us -> 96.9 us  [per_device(): pl.pallas_call(kernel, out_shape=shapes, in_specs=[pl.BlockSpec(memory_sp...]
where the time goes in v3:
time: 101 us
  Pallas kernels  98 us (97%)
  local copies, waits for them, and re-layouts  1.89 us (2%)
    pallas_call x1, Pallas kernels, per_device(): pl.pallas_call(kernel, out_shape=shapes, in_specs=[pl.BlockSpec(memory_sp...  96.9 us

profile of v3, /device:TPU:4, one launch (start us, length us, event | category | flops | bytes accessed | tf_op | source)
XLA Modules:
  0.0 100.5 jit_solution(13495922945558569959)
XLA Ops:
  0.6 0.0 copy-start
  0.6 0.9 copy-done
  1.6 0.0 copy-start.1
  1.6 0.9 copy-done.1
  2.5 96.9 %log_sparse_attention.1 = (bf16[256,512]{1,0:T(8,128)(2,1)S(1)}, bf16[256,512]{1,0:T(8,128)(2,1)S(1)}, bf16[256,512]{1,0:T(8,128)(2,1)S(1)}, bf16[256,512]{1,0:T(8,128)(2,1)S(1)}, f32[128,512]{1,0:T(8,128)S(1)}) custom-call(bf16[256,512]{1,0:T(8,128)(2,1)S(1)} %copy-done, bf16[256,512]{1,0:T(8,128)(2,1)S(1)} %copy-done.1, bf16[256,512]{1,0:T(8,128)(2,1)} %v_in.1, ...), custom_call_target="tpu_custom_call" | custom-call | flops 5000000000 | bytes 10000000 | tf_op jit(solution)/shard_map/log_sparse_attention/pallas_call | solution.py:476
  99.4 1.1 %hand_over.1 = (bf16[256,512]{1,0:T(8,128)(2,1)}, bf16[256,512]{1,0:T(8,128)(2,1)}, bf16[256,512]{1,0:T(8,128)(2,1)}, bf16[256,512]{1,0:T(8,128)(2,1)}, f32[128,512]{1,0:T(8,128)}) custom-call(bf16[256,512]{1,0:T(8,128)(2,1)S(1)} %get-tuple-element.10.refs_0_, bf16[256,512]{1,0:T(8,128)(2,1)S(1)} %get-tuple-element.11.refs_1_, ...), custom_call_target="tpu_custom_call" | custom-call | tf_op jit(solution)/shard_map/hand_over/pallas_call | solution.py:518
Async XLA Ops:
  0.6 1.0 copy-start
  1.6 0.9 copy-start.1

commit v4 on v3

--- a/solution.py
+++ b/solution.py
@@ -276,7 +276,7 @@
         for s in range(1, XS):
             at_copy(s, j).start()
         row_dots = jnp.sum(cg.astype(F32).T * att_t, axis=0, keepdims=True)
-        for lv in range(LV):
+        for lv in (3, 5, 2, 4, 1, 0):
             normed = sc[lv] * inverse
             prob_grad = dot_nt(kv[j, 1, lv], cg)
             ds = (normed * (prob_grad - row_dots)).astype(BF16)
@@ -510,7 +510,7 @@
             dma((GROUPS, 2, UP)), dma((GROUPS, 2, UP)),
         ],
         compiler_params=pltpu.CompilerParams(
-            collective_id=0, has_side_effects=True, vmem_limit_bytes=52 * 1024 * 1024
+            collective_id=0, has_side_effects=True, vmem_limit_bytes=52 * 1024 * 1024 + 512 * 1024
         ),
         cost_estimate=pl.CostEstimate(flops=5 * 10**9, bytes_accessed=10**7, transcendentals=2 * 10**6),
         name="log_sparse_attention",

time: 101 us -> 98.3 us (0.973)
  local copies, waits for them, and re-layouts: 1.89 us -> 0 us
    unnamed x4 -> x0, local copies, waits for them, and re-layouts: 1.89 us -> none
where the time goes in v4:
time: 98.3 us; the launch traced here: 98.2 us
  Pallas kernels  97.6 us (99%)
    pallas_call x1, Pallas kernels, per_device(): pl.pallas_call(kernel, out_shape=shapes, in_specs=[pl.BlockSpec(memory_sp...  96.5 us

profile of v4, /device:TPU:4, one launch (start us, length us, event | category | flops | bytes accessed | tf_op | source)
XLA Modules:
  0.0 98.2 jit_solution(8728862403746520230)
XLA Ops:
  0.6 96.5 %log_sparse_attention.1 = (bf16[256,512]{1,0:T(8,128)(2,1)S(1)}, bf16[256,512]{1,0:T(8,128)(2,1)S(1)}, bf16[256,512]{1,0:T(8,128)(2,1)S(1)}, bf16[256,512]{1,0:T(8,128)(2,1)S(1)}, f32[128,512]{1,0:T(8,128)S(1)}) custom-call(bf16[256,512]{1,0:T(8,128)(2,1)} %q_in.1, bf16[256,512]{1,0:T(8,128)(2,1)} %k_in.1, bf16[256,512]{1,0:T(8,128)(2,1)} %v_in.1, ...), custom_call_target="tpu_custom_call" | custom-call | flops 5000000000 | bytes 10000000 | tf_op jit(solution)/shard_map/log_sparse_attention/pallas_call | solution.py:476
  97.1 1.1 %hand_over.1 = (bf16[256,512]{1,0:T(8,128)(2,1)}, bf16[256,512]{1,0:T(8,128)(2,1)}, bf16[256,512]{1,0:T(8,128)(2,1)}, bf16[256,512]{1,0:T(8,128)(2,1)}, f32[128,512]{1,0:T(8,128)}) custom-call(bf16[256,512]{1,0:T(8,128)(2,1)S(1)} %get-tuple-element.10.refs_0_, bf16[256,512]{1,0:T(8,128)(2,1)S(1)} %get-tuple-element.11.refs_1_, ...), custom_call_target="tpu_custom_call" | custom-call | tf_op jit(solution)/shard_map/hand_over/pallas_call | solution.py:518

commit v5 on v4

--- a/solution.py
+++ b/solution.py
@@ -19,6 +19,7 @@
 XS = 4
 UP = 4
 DOWN = 3
+RISE = 2
 GROUPS = 2
 WIDE = FEAT // GROUPS
 HP = 8
@@ -148,6 +149,9 @@
         pl.semaphore_signal(barrier, inc=1, device_id=peer, device_id_type=MESH)
     pl.semaphore_wait(barrier, len(peers))
 
+    for s in range(1, XS):
+        fy_copy(s).start()
+    fc_copy(0).start()
     for j in range(HEADS):
         local_copy(0, j).wait()
         local_copy(1, j).wait()
@@ -161,10 +165,6 @@
                 nk_copy(j, 0).start()
 
         kv_copy(4, j).start()
-        if j == 0:
-            fc_copy(0).start()
-            for s in range(1, XS):
-                fy_copy(s).start()
 
     def relay_near(j):
         kv_copy(4, j).wait_recv()
@@ -289,18 +289,18 @@
                 if lv == 5:
                     gr_copy(lv, j).start()
                 else:
-                    @pl.when(j < 2)
+                    @pl.when(j < RISE)
                     def _():
                         gr_copy(3, j).start()
 
-                    @pl.when(j >= 2)
+                    @pl.when(j >= RISE)
                     def _():
                         gn_copy(j).start()
             else:
                 own[lv, j, 0] = dk
                 own[lv, j, 1] = dv
                 if lv == 2:
-                    @pl.when(j >= 2)
+                    @pl.when(j >= RISE)
                     def _():
                         gs[1, j, 0] = dk.astype(BF16)
                         gs[1, j, 1] = dv.astype(BF16)
@@ -326,7 +326,7 @@
     upper = (z >= ZS // 2).astype(F32)
 
     def eight(j):
-        if j < 2:
+        if j < RISE:
             pass_on(5, 4, j)
         else:
             gr_copy(5, j).wait_recv()
@@ -339,7 +339,7 @@
         gr_copy(1, j).wait_recv()
         gr_copy(4, j).wait_recv()
         total = own[0, j] + gr[0, j].astype(F32) + gr[3, j].astype(F32)
-        if j >= 2:
+        if j >= RISE:
             total = total + (1.0 - upper) * gr[2, j].astype(F32)
         dk_o[:, cols(j, HDIM)] = total[0].astype(BF16)
         dv_o[:, cols(j, HDIM)] = total[1].astype(BF16)
@@ -380,11 +380,11 @@
                 wo_o[:, g * WIDE : (g + 1) * WIDE] = part[g, z] + wor[g, way, k - 1].astype(F32)
 
     relay_near(0)
+    relay_near(1)
     relay_down(0)
-    relay_near(1)
     pass_upstream()
+    relay_near(2)
     relay_down(1)
-    relay_near(2)
     exchange_columns()
     relay_near(3)
     context()
@@ -393,11 +393,8 @@
     def stage(t, carry):
         @pl.when(t == 1)
         def _():
+            spread_columns()
             relay_up(3)
-
-        @pl.when(t == 2)
-        def _():
-            spread_columns()
 
         @pl.when(t == 3)
         def _():
@@ -410,29 +407,29 @@
     chain_one(1)
     send_up(2)
     finish_columns()
+    project(1)
+    project(0)
+    eight(0)
+    chain_two(0)
+    eight(1)
+    chain_two(1)
+    ring(1, 1)
+    ring(0, 1)
+    send_up(3)
     chain_two(2)
-    project(0)
-    project(1)
-    eight(1)
-    chain_two(0)
-    ring(0, 1)
-    ring(1, 1)
-    send_up(3)
+    ring(1, 2)
     eight(2)
-    chain_two(1)
     ring(0, 2)
-    ring(1, 2)
-    eight(0)
+    eight(3)
+    chain_two(3)
+    ring(1, 3)
+    ring(0, 3)
+    last(2)
     last(1)
-    chain_two(3)
-    eight(3)
-    ring(0, 3)
-    ring(1, 3)
     last(0)
-    last(2)
+    ring(1, 4)
+    last(3)
     ring(0, 4)
-    last(3)
-    ring(1, 4)
 
     def drain(j, carry):
         for lv in range(1, LV):
@@ -445,7 +442,8 @@
     lax.fori_loop(0, HEADS, drain, 0)
     for j in (0, 1):
         nk_copy(j, 0).wait_send()
-        gn_copy(j + 2).wait_send()
+        if j + 2 >= RISE:
+            gn_copy(j + 2).wait_send()
     for g in range(GROUPS):
         for way, steps in ((0, UP), (1, DOWN)):
             for k in range(steps):

time: 98.3 us -> 96.2 us (0.979)
  Pallas kernels: 97.6 us -> 95.4 us
    pallas_call x1, Pallas kernels: 96.5 us -> 94.3 us  [per_device(): pl.pallas_call(kernel, out_shape=shapes, in_specs=[pl.BlockSpec(memory_sp...]
where the time goes in v5:
time: 96.2 us; the launch traced here: 96.1 us
  Pallas kernels  95.4 us (99%)
    pallas_call x1, Pallas kernels, per_device(): pl.pallas_call(kernel, out_shape=shapes, in_specs=[pl.BlockSpec(memory_sp...  94.3 us

profile of v5, /device:TPU:4, one launch (start us, length us, event | category | flops | bytes accessed | tf_op | source)
XLA Modules:
  0.0 96.1 jit_solution(13207189405355949310)
XLA Ops:
  0.6 94.3 %log_sparse_attention.1 = (bf16[256,512]{1,0:T(8,128)(2,1)S(1)}, bf16[256,512]{1,0:T(8,128)(2,1)S(1)}, bf16[256,512]{1,0:T(8,128)(2,1)S(1)}, bf16[256,512]{1,0:T(8,128)(2,1)S(1)}, f32[128,512]{1,0:T(8,128)S(1)}) custom-call(bf16[256,512]{1,0:T(8,128)(2,1)} %q_in.1, bf16[256,512]{1,0:T(8,128)(2,1)} %k_in.1, bf16[256,512]{1,0:T(8,128)(2,1)} %v_in.1, ...), custom_call_target="tpu_custom_call" | custom-call | flops 5000000000 | bytes 10000000 | tf_op jit(solution)/shard_map/log_sparse_attention/pallas_call | solution.py:474
  95.0 1.1 %hand_over.1 = (bf16[256,512]{1,0:T(8,128)(2,1)}, bf16[256,512]{1,0:T(8,128)(2,1)}, bf16[256,512]{1,0:T(8,128)(2,1)}, bf16[256,512]{1,0:T(8,128)(2,1)}, f32[128,512]{1,0:T(8,128)}) custom-call(bf16[256,512]{1,0:T(8,128)(2,1)S(1)} %get-tuple-element.10.refs_0_, bf16[256,512]{1,0:T(8,128)(2,1)S(1)} %get-tuple-element.11.refs_1_, ...), custom_call_target="tpu_custom_call" | custom-call | tf_op jit(solution)/shard_map/hand_over/pallas_call | solution.py:516

commit v6 on v5

--- a/solution.py
+++ b/solution.py
@@ -405,31 +405,31 @@
 
     lax.fori_loop(0, HEADS, stage, 0)
     chain_one(1)
+    eight(0)
     send_up(2)
     finish_columns()
+    chain_two(0)
     project(1)
     project(0)
-    eight(0)
-    chain_two(0)
-    eight(1)
     chain_two(1)
     ring(1, 1)
     ring(0, 1)
     send_up(3)
+    eight(1)
+    eight(2)
     chain_two(2)
+    ring(0, 2)
     ring(1, 2)
-    eight(2)
-    ring(0, 2)
+    chain_two(3)
+    last(0)
     eight(3)
-    chain_two(3)
+    last(2)
+    ring(0, 3)
     ring(1, 3)
-    ring(0, 3)
-    last(2)
     last(1)
-    last(0)
+    ring(0, 4)
+    last(3)
     ring(1, 4)
-    last(3)
-    ring(0, 4)
 
     def drain(j, carry):
         for lv in range(1, LV):

time: 96.2 us -> 101 us (1.050)
  Pallas kernels: 95.4 us -> 100 us
    pallas_call x1, Pallas kernels: 94.3 us -> 99.3 us  [per_device(): pl.pallas_call(kernel, out_shape=shapes, in_specs=[pl.BlockSpec(memory_sp...]
where the time goes in v6:
time: 101 us
  Pallas kernels  100 us (99%)
    pallas_call x1, Pallas kernels, per_device(): pl.pallas_call(kernel, out_shape=shapes, in_specs=[pl.BlockSpec(memory_sp...  99.3 us

profile of v6, /device:TPU:4, one launch (start us, length us, event | category | flops | bytes accessed | tf_op | source)
XLA Modules:
  0.0 101.1 jit_solution(299807903531968960)
XLA Ops:
  0.6 99.3 %log_sparse_attention.1 = (bf16[256,512]{1,0:T(8,128)(2,1)S(1)}, bf16[256,512]{1,0:T(8,128)(2,1)S(1)}, bf16[256,512]{1,0:T(8,128)(2,1)S(1)}, bf16[256,512]{1,0:T(8,128)(2,1)S(1)}, f32[128,512]{1,0:T(8,128)S(1)}) custom-call(bf16[256,512]{1,0:T(8,128)(2,1)} %q_in.1, bf16[256,512]{1,0:T(8,128)(2,1)} %k_in.1, bf16[256,512]{1,0:T(8,128)(2,1)} %v_in.1, ...), custom_call_target="tpu_custom_call" | custom-call | flops 5000000000 | bytes 10000000 | tf_op jit(solution)/shard_map/log_sparse_attention/pallas_call | solution.py:474
  100.0 1.1 %hand_over.1 = (bf16[256,512]{1,0:T(8,128)(2,1)}, bf16[256,512]{1,0:T(8,128)(2,1)}, bf16[256,512]{1,0:T(8,128)(2,1)}, bf16[256,512]{1,0:T(8,128)(2,1)}, f32[128,512]{1,0:T(8,128)}) custom-call(bf16[256,512]{1,0:T(8,128)(2,1)S(1)} %get-tuple-element.10.refs_0_, bf16[256,512]{1,0:T(8,128)(2,1)S(1)} %get-tuple-element.11.refs_1_, ...), custom_call_target="tpu_custom_call" | custom-call | tf_op jit(solution)/shard_map/hand_over/pallas_call | solution.py:516
